TPU v7x, 256 devices: a whole 4x4x8 slice. The times are simulated.
256 devices in a mesh: dp: 256 (over x, y, z, core).
Axes of the slice: x: 4, y: 4, z: 8, core: 2. Of those that a mesh axis runs over, the one named last changes fastest.
Arguments:
- images: bfloat16 [262144, 1152], P('dp'), may hold values from -0.1875 to 0.1875
- texts: bfloat16 [262144, 1152], P('dp'), may hold values from -0.1875 to 0.1875
- positive: int32 [262144], P('dp'), may hold values from 0 to 262143, as said below
- loss_cotangent: float32 [], replicated, may hold values from 256 to 1024
Outputs:
- image_grad: bfloat16 [262144, 1152], P('dp')
- text_grad: float32 [262144, 1152], P('dp')
Inputs may be any that keep to these rules, and one draw needn't show every extreme that they name: `positive`: the 1024 rows of each block name every text row of that same block exactly once.
All inputs are finite; a program needn't handle non-finite values.
Results may differ from a plain program's by a relative error of at most 0.005.
Values may be sent and summed in bfloat16 or wider, within the bound.
No kernel may reach another device: no remote copies, remote signals or barrier semaphores. Data moves between devices by JAX's collectives and lax.ppermute only.
A program may use at most 64 MiB of HBM per device.

v0:
```python
import jax
import jax.numpy as jnp
from jax import lax
from jax.sharding import PartitionSpec as P

LOGIT_SCALE = 10.0
SCORE_OFFSET = -2.0


def passed_along(shard, axis, by):
    size = lax.axis_size(axis)
    return lax.ppermute(shard, axis, [(i, (i + by) % size) for i in range(size)])


def logit_tile(image_rows, text_rows):
    return (
        LOGIT_SCALE
        * jnp.einsum("id,jd->ij", image_rows, text_rows, preferred_element_type=jnp.float32)
        + SCORE_OFFSET
    )


def text_terms(coefficients, image_rows):
    return jnp.einsum("ij,id->jd", coefficients, image_rows, preferred_element_type=jnp.float32)


def local(images, texts, positive, loss_cotangent):
    total_rows = images.shape[0]
    scale_factor = loss_cotangent * (LOGIT_SCALE / total_rows)
    first_row = lax.axis_index("dp") * total_rows
    local_match = positive - first_row
    columns = jnp.arange(total_rows, dtype=jnp.int32)
    labels = (local_match[:, None] == columns[None, :]).astype(jnp.float32)
    prior_texts = passed_along(texts, "dp", 1)
    own_coef = (jax.nn.sigmoid(logit_tile(images, texts)) - labels).astype(jnp.bfloat16)
    own_text = scale_factor * text_terms(own_coef, images)
    far_coef = jax.nn.sigmoid(logit_tile(images, prior_texts)).astype(jnp.bfloat16)
    image_sum = jnp.dot(own_coef, texts, preferred_element_type=jnp.float32) + jnp.dot(
        far_coef, prior_texts, preferred_element_type=jnp.float32
    )
    image_grad = (scale_factor * image_sum).astype(jnp.bfloat16)
    travel = scale_factor * text_terms(far_coef, images)
    text_grad = own_text + passed_along(travel.astype(jnp.bfloat16), "dp", -1).astype(travel.dtype)
    return (image_grad, text_grad)


def solution(mesh):
    in_specs = (P("dp", None), P("dp", None), P("dp"), P())
    out_specs = (P("dp", None), P("dp", None))
    return jax.shard_map(local, mesh=mesh, in_specs=in_specs, out_specs=out_specs, check_vma=False)
```

profile of v0, /device:TPU:0, one launch (start us, length us, event | category | flops | bytes accessed | tf_op | source)
XLA Modules:
  0.0 75.4 jit_solution(13216315678490090288)
XLA Ops:
  0.6 0.0 copy-start
  0.6 0.1 collective-permute-start
  1.5 0.7 broadcast_subtract_fusion
  2.2 33.5 %collective-permute-done = bf16[1024,1152]{1,0:T(8,128)(2,1)} collective-permute-done((bf16[1024,1152]{1,0:T(8,128)(2,1)}, bf16[1024,1152]{1,0:T(8,128)(2,1)}, u32[]{:S(2)}, u32[]{:S(2)}) %collective-permute-start) | collective-permute-done | bytes 2359328 | tf_op jit(solution)/shard_map/ppermute | solution.py:12
  35.8 0.0 copy-done
  35.8 5.3 %divide_convert_fusion = bf16[1024,1024]{1,0:T(8,128)(2,1)S(1)} fusion(bf16[1024,1152]{1,0:T(8,128)(2,1)S(1)} %copy-done, bf16[1024,1152]{1,0:T(8,128)(2,1)} %collective-permute-done), kind=kOutput, calls=%fused_computation.4 | convolution fusion | flops 2422210560 | bytes 6815744 | tf_op jit(solution)/shard_map/id,jd->ij/dot_general | solution.py:18
  41.1 0.0 copy-start.1
  41.1 3.2 %fusion = bf16[1024,1152]{1,0:T(8,128)(2,1)S(1)} fusion(bf16[1024,1024]{1,0:T(8,128)(2,1)S(1)} %divide_convert_fusion, bf16[1024,1152]{1,0:T(8,128)(2,1)S(1)} %copy-done, f32[]{:T(128)S(6)} %mul.26), kind=kOutput, calls=%fused_computation.7 | convolution fusion | flops 2418278400 | bytes 6815748 | tf_op jit(solution)/shard_map/ij,id->jd/dot_general | solution.py:24
  44.3 0.1 collective-permute-start.1
  44.4 0.0 copy-done.1
  44.4 3.9 %subtract_convert_fusion = bf16[1024,1024]{1,0:T(8,128)(2,1)S(1)} fusion(bf16[1024,1152]{1,0:T(8,128)(2,1)S(1)} %copy-done, bf16[1024,1152]{1,0:T(8,128)(2,1)S(1)} %copy-done.1, s32[1024]{0:T(1024)S(1)} %broadcast_subtract_fusion), kind=kOutput, calls=%fused_computation.5 | convolution fusion | flops 2425356288 | bytes 6819840 | tf_op jit(solution)/shard_map/id,jd->ij/dot_general | solution.py:18
  48.3 2.9 %fusion.1 = f32[1024,1152]{1,0:T(8,128)S(1)} fusion(bf16[1024,1024]{1,0:T(8,128)(2,1)S(1)} %subtract_convert_fusion, bf16[1024,1152]{1,0:T(8,128)(2,1)S(1)} %copy-done.1), kind=kOutput, calls=%fused_computation.9 | convolution fusion | flops 2415919104 | bytes 9175040 | tf_op jit(solution)/shard_map/dot_general | solution.py:38
  51.2 5.8 %multiply_convert_fusion = bf16[1024,1152]{1,0:T(8,128)(2,1)} fusion(f32[1024,1152]{1,0:T(8,128)S(1)} %fusion.1, bf16[1024,1024]{1,0:T(8,128)(2,1)S(1)} %divide_convert_fusion, bf16[1024,1152]{1,0:T(8,128)(2,1)} %collective-permute-done, f32[]{:T(128)S(6)} %mul.26), kind=kOutput, calls=%fused_computation.3 | convolution fusion | flops 2419458048 | bytes 11534340 | tf_op jit(solution)/shard_map/dot_general | solution.py:38
  57.0 13.7 %collective-permute-done.1 = bf16[1024,1152]{1,0:T(8,128)(2,1)S(1)} collective-permute-done((bf16[1024,1152]{1,0:T(8,128)(2,1)S(1)}, bf16[1024,1152]{1,0:T(8,128)(2,1)S(1)}, u32[]{:S(2)}, u32[]{:S(2)}) %collective-permute-start.1) | collective-permute-done | bytes 2359328 | tf_op jit(solution)/shard_map/ppermute | solution.py:12
  70.7 4.6 %convert_add_fusion = f32[1024,1152]{1,0:T(8,128)} fusion(bf16[1024,1152]{1,0:T(8,128)(2,1)S(1)} %collective-permute-done.1, bf16[1024,1024]{1,0:T(8,128)(2,1)S(1)} %subtract_convert_fusion, bf16[1024,1152]{1,0:T(8,128)(2,1)S(1)} %copy-done, f32[]{:T(128)S(6)} %mul.26), kind=kOutput, calls=%fused_computation.2 | convolution fusion | flops 2419458048 | bytes 11534340 | tf_op jit(solution)/shard_map/ij,id->jd/dot_general | solution.py:24
Async XLA Ops:
  0.6 35.1 %copy-start = (bf16[1024,1152]{1,0:T(8,128)(2,1)S(1)}, bf16[1024,1152]{1,0:T(8,128)(2,1)}, u32[]{:S(2)}) copy-start(bf16[1024,1152]{1,0:T(8,128)(2,1)} %param.4) | copy-start | bytes 7077892
  0.6 35.1 %collective-permute-start = (bf16[1024,1152]{1,0:T(8,128)(2,1)}, bf16[1024,1152]{1,0:T(8,128)(2,1)}, u32[]{:S(2)}, u32[]{:S(2)}) collective-permute-start(bf16[1024,1152]{1,0:T(8,128)(2,1)} %param.5), channel_id=1, source_target_pairs={{0,1},{1,2},{2,3},{3,4},{4,5},{5,6},{6,7},{7,8},{8,9},{9,10},{10,1... | collective-permute-start | bytes 7077896 | tf_op jit(solution)/shard_map/ppermute | solution.py:12
  41.1 3.3 %copy-start.1 = (bf16[1024,1152]{1,0:T(8,128)(2,1)S(1)}, bf16[1024,1152]{1,0:T(8,128)(2,1)}, u32[]{:S(2)}) copy-start(bf16[1024,1152]{1,0:T(8,128)(2,1)} %param.5) | copy-start | bytes 7077892
  44.3 26.4 %collective-permute-start.1 = (bf16[1024,1152]{1,0:T(8,128)(2,1)S(1)}, bf16[1024,1152]{1,0:T(8,128)(2,1)S(1)}, u32[]{:S(2)}, u32[]{:S(2)}) collective-permute-start(bf16[1024,1152]{1,0:T(8,128)(2,1)S(1)} %fusion), channel_id=1, source_target_pairs={{0,255},{1,0},{2,1},{3,2},{4,3},{5,4},{6,5},{7,6},{8,7},{9,8},{10,... | collective-permute-start | bytes 7077896 | tf_op jit(solution)/shard_map/ppermute | solution.py:12
where the time goes:
time: 75.6 us; the launch traced here: 75.4 us
  waiting for transfers between devices  47.3 us (63%)
  matrix products  25.7 us (34%)
  between operations  1.5 us (2%)
    ppermute x2, waiting for transfers between devices, passed_along(): lax.ppermute(shard, axis, [(i, (i + by) % size) for i in range(size)])  47.3 us
    dot_general x2, matrix products, logit_tile(): jnp.einsum('id,jd->ij', image_rows, text_rows, preferred_element_type=jnp...  9.14 us
    dot_general x2, matrix products, text_terms(): jnp.einsum('ij,id->jd', coefficients, image_rows, preferred_element_type=...  7.86 us
    dot_general x1, matrix products, local(): jnp.dot(far_coef, prior_texts, preferred_element_type=jnp.float32)  5.84 us
    dot_general x1, matrix products, local(): jnp.dot(own_coef, texts, preferred_element_type=jnp.float32)  2.87 us
  transfers between devices with their start and end apart: 2, of which 2 were waited for; matrix products, arithmetic and copies ran while one was open for 18% of the time, Pallas kernels for 0%

commit v1 on v0

v1 whole, which is shorter than its diff:
```python
import functools
import math

import jax
import jax.numpy as jnp
from jax import lax
from jax.experimental import pallas as pl
from jax.experimental.pallas import tpu as pltpu
from jax.sharding import PartitionSpec as P

LOGIT_SCALE = 10.0
SCORE_OFFSET = -2.0
FAR_ROWS = (768, 256)
NEAR_ROWS = (512, 512)
OWN_TILE = 256
PICK_TILE = 128
PAIR_TILE = 512
NT = (((1,), (1,)), ((), ()))
NN = (((1,), (0,)), ((), ()))
TN = (((0,), (0,)), ((), ()))
VMEM = pl.BlockSpec(memory_space=pltpu.VMEM)
SMEM = pl.BlockSpec(memory_space=pltpu.SMEM)
ANY = pl.BlockSpec(memory_space=pl.ANY)


def mm(a, b, dims):
    return lax.dot_general(a, b, dims, preferred_element_type=jnp.float32)


def sigmoid(product):
    per_bit = 1.0 / math.log(2.0)
    return 1.0 / (1.0 + jnp.exp2(product * (-LOGIT_SCALE * per_bit) - SCORE_OFFSET * per_bit))


def in_vmem(x):
    return pltpu.with_memory_space_constraint(x, pltpu.VMEM)


def in_hbm(x):
    return pltpu.with_memory_space_constraint(x, pltpu.HBM)


def params(mib):
    return pltpu.CompilerParams(vmem_limit_bytes=mib << 20)


def cost(matmuls, rows, cols, depth):
    return pl.CostEstimate(flops=2 * matmuls * rows * cols * depth, bytes_accessed=0, transcendentals=0)


def is_even():
    return lax.rem(lax.axis_index("dp"), 2) == 0


def pick_kernel(starts, scaled, images_ref, texts_ref, *refs):
    n = len(starts)
    outs, sems = refs[-n - 1 : -1], refs[-1]
    if scaled:
        cotangent_ref, scale_ref = refs[0], refs[-n - 2]
    even = is_even()

    def copies(i, source):
        start, total = starts[i][0], outs[i].shape[0]
        return [
            pltpu.make_async_copy(
                source.at[pl.ds(start + at, PICK_TILE), :], outs[i].at[pl.ds(at, PICK_TILE), :], sems.at[i, at // PICK_TILE]
            )
            for at in range(0, total, PICK_TILE)
        ]

    def begin(flipped):
        for i, (_, flip) in enumerate(starts):
            for copy in copies(i, images_ref if flip == flipped else texts_ref):
                copy.start()

    @pl.when(even)
    def _():
        begin(False)

    @pl.when(jnp.logical_not(even))
    def _():
        begin(True)

    for i in range(n):
        for copy in copies(i, images_ref):
            copy.wait()
    if scaled:
        total = images_ref.shape[0]
        scale_ref[...] = jnp.full(scale_ref.shape, cotangent_ref[0] * (LOGIT_SCALE / total), jnp.float32)


def pick(images, texts, wanted, cotangent=None, after=()):
    depth = images.shape[1]
    n = len(wanted)
    scale = () if cotangent is None else (pltpu.VMEM((8, depth), jnp.float32),)
    return pl.pallas_call(
        functools.partial(pick_kernel, [(w[0], w[2]) for w in wanted], bool(scale)),
        out_shape=scale + tuple(pltpu.VMEM((w[1], depth), images.dtype) for w in wanted),
        in_specs=[ANY] * 2 + [SMEM] * len(scale) + [ANY] * len(after),
        out_specs=(VMEM,) * (n + len(scale)),
        scratch_shapes=[pltpu.SemaphoreType.DMA((n, max(w[1] for w in wanted) // PICK_TILE))],
        compiler_params=params(6),
        cost_estimate=pl.CostEstimate(flops=0, bytes_accessed=4 * depth * sum(w[1] for w in wanted), transcendentals=0),
    )(in_hbm(images), in_hbm(texts), *([] if cotangent is None else [cotangent]), *after)


def across(coef, others):
    total, at = None, 0
    for other in others:
        part = mm(coef[:, at : at + other.shape[0]], other, NN)
        total = part if total is None else total + part
        at += other.shape[0]
    return total


def own_kernel(chunks, match_ref, *refs):
    a_refs, b_refs, (acc_a, acc_b) = refs[:chunks], refs[chunks:-2], refs[-2:]
    rows = acc_b.shape[0]
    even = is_even()
    first = lax.axis_index("dp") * rows
    match_row = match_ref[...] - first
    others = [ref[...] for ref in b_refs]
    tiles = [(ref, start) for ref in a_refs for start in range(0, ref.shape[0], OWN_TILE)]

    def load(t):
        ref, start = tiles[t]
        return ref[start : start + OWN_TILE, :]

    def product_of(t):
        return jnp.concatenate([mm(load(t), other, NT) for other in others], axis=1)

    product = product_of(0)
    for t in range(len(tiles)):
        at = t * OWN_TILE
        if t + 1 < len(tiles):
            following = product_of(t + 1)
        match_tile = jnp.broadcast_to(match_ref[:, at : at + OWN_TILE] - first, (128, OWN_TILE)).T
        match_col = jnp.concatenate([match_tile] * (rows // 128), axis=1)
        lane = lax.broadcasted_iota(jnp.int32, (OWN_TILE, rows), 1)
        row = lax.broadcasted_iota(jnp.int32, (OWN_TILE, rows), 0) + at
        gap = jnp.where(even, match_col - lane, match_row - row)
        coef = (sigmoid(product) - jnp.where(gap == 0, 1.0, 0.0)).astype(jnp.bfloat16)
        acc_a[at : at + OWN_TILE, :] = across(coef, others)
        term = mm(coef, load(t), TN)
        if t == 0:
            acc_b[...] = term
        else:
            acc_b[...] += term
        product = following

def own_tile(own, base, match):
    rows, depth = sum(o.shape[0] for o in base), base[0].shape[1]
    n = len(own)
    return pl.pallas_call(
        functools.partial(own_kernel, n),
        out_shape=(
            pltpu.VMEM((rows, depth), jnp.float32),
            pltpu.VMEM((rows, depth), jnp.float32),
        ),
        in_specs=[VMEM] * (n + 1 + len(base)),
        out_specs=(VMEM, VMEM),
        compiler_params=params(20),
        cost_estimate=cost(3, rows, rows, depth),
    )(in_vmem(match), *[in_vmem(o) for o in own], *[in_vmem(o) for o in base])


def pair_tiles(own_refs, other_refs, tile):
    tiles = [(ref, start) for ref in own_refs for start in range(0, ref.shape[0], tile)]
    sizes = [min(tile, ref.shape[0] - start) for ref, start in tiles]
    others = [ref[...] for ref in other_refs]

    def products(t):
        ref, start = tiles[t]
        own = ref[start : start + sizes[t], :]
        return [mm(own, other, NT) for other in others]

    at, held = 0, products(0)
    for t in range(len(tiles)):
        following = products(t + 1) if t + 1 < len(tiles) else None
        term = None
        for product, other in zip(held, others, strict=True):
            part = mm(sigmoid(product).astype(jnp.bfloat16), other, NN)
            term = part if term is None else term + part
        yield t, at, sizes[t], term
        at += sizes[t]
        held = following


def last_kernel(chunks, parts, to_image, tile, *refs):
    own_refs, other_refs, rest = refs[:chunks], refs[chunks : chunks + parts], refs[chunks + parts :]
    acc_ref, scale_ref = rest[:2]
    image_ref, text_ref, wide, narrow, sems = rest[-5:]
    even = is_even()

    def go(stage, out_ref):
        scale = scale_ref[0:1, :]
        copies = []
        for t, at, size, term in pair_tiles(own_refs, other_refs, tile):
            rows = pl.ds(at, size)
            stage[rows, :] = (scale * (acc_ref[rows, :] + term)).astype(stage.dtype)
            copies.append(pltpu.make_async_copy(stage.at[rows, :], out_ref.at[rows, :], sems.at[t]))
            copies[-1].start()
        for copy in copies:
            copy.wait()

    @pl.when(even == to_image)
    def _():
        go(narrow, image_ref)

    @pl.when(even != to_image)
    def _():
        go(wide, text_ref)


def last(own, other, acc, scale, outs, to_image):
    rows, depth = acc.shape
    given = [] if outs is None else list(outs)
    n, parts = len(own), len(other)
    return pl.pallas_call(
        functools.partial(last_kernel, n, parts, to_image, PAIR_TILE),
        out_shape=(
            jax.ShapeDtypeStruct((rows, depth), jnp.bfloat16),
            jax.ShapeDtypeStruct((rows, depth), jnp.float32),
        ),
        in_specs=[VMEM] * (n + parts + 2) + [ANY] * len(given),
        out_specs=(ANY, ANY),
        scratch_shapes=[
            pltpu.VMEM((rows, depth), jnp.float32),
            pltpu.VMEM((rows, depth), jnp.bfloat16),
            pltpu.SemaphoreType.DMA((8,)),
        ],
        input_output_aliases={n + parts + 2 + i: i for i in range(len(given))},
        compiler_params=params(20),
        cost_estimate=cost(2, rows, sum(o.shape[0] for o in other), depth),
    )(*[in_vmem(o) for o in own], *[in_vmem(o) for o in other], in_vmem(acc), in_vmem(scale), *given)


def middle_kernel(chunks, *refs):
    own_refs, other_ref, acc_ref, out_ref = refs[:chunks], refs[chunks], refs[chunks + 1], refs[-1]
    for _, at, size, term in pair_tiles(own_refs, [other_ref], PAIR_TILE):
        rows = pl.ds(at, size)
        out_ref[rows, :] = acc_ref[rows, :] + term


def middle(own, other, acc, after):
    rows, depth = acc.shape
    n = len(own)
    return pl.pallas_call(
        functools.partial(middle_kernel, n),
        out_shape=pltpu.VMEM((rows, depth), jnp.float32),
        in_specs=[VMEM] * (n + 2) + [ANY] * len(after),
        out_specs=VMEM,
        input_output_aliases={n + 1: 0},
        compiler_params=params(16),
        cost_estimate=cost(2, rows, other.shape[0], depth),
    )(*[in_vmem(o) for o in own], in_vmem(other), in_vmem(acc), *[in_hbm(o) for o in after])


def spans(counts, flip):
    start = 0
    for count in counts:
        yield start, count, flip
        start += count


def local(images, texts, positive, loss_cotangent):
    rows = images.shape[0]
    size = lax.axis_size("dp")
    far_pairs = [(p, (p - 1) % size if p % 2 == 0 else (p + 1) % size) for p in range(size)]
    near_pairs = [(p, p + 1 if p % 2 == 0 else p - 1) for p in range(size)]
    (first,) = pick(images, texts, [(0, FAR_ROWS[0], False)])
    wanted = list(spans(FAR_ROWS, False))[1:] + list(spans(NEAR_ROWS, True))
    cotangent, first = lax.optimization_barrier((loss_cotangent, first))
    scale, *picked = pick(images, texts, wanted, cotangent.reshape(1), (first,))
    far_own, near_own = [first, *picked[: len(FAR_ROWS) - 1]], picked[len(FAR_ROWS) - 1 :]
    far = [lax.ppermute(part, "dp", far_pairs) for part in far_own]
    near = [lax.ppermute(part, "dp", near_pairs) for part in near_own]
    far_acc, near_acc = own_tile(far_own, near_own, positive.reshape(1, rows))
    outs = last(near_own, near, near_acc, scale, None, False)
    for part in far[:-1]:
        far_acc = middle(far_own, part, far_acc, outs)
    return last(far_own, far[-1:], far_acc, scale, outs, True)


def solution(mesh):
    in_specs = (P("dp", None), P("dp", None), P("dp"), P())
    out_specs = (P("dp", None), P("dp", None))
    return jax.shard_map(local, mesh=mesh, in_specs=in_specs, out_specs=out_specs, check_vma=False)
```

time: 75.6 us -> 41.3 us (0.55)
  the two profiles are of different devices: /device:TPU:0 before, /device:TPU:1 now
where the time goes in v1:
time: 41.3 us; the launch traced here: 41.2 us
  Pallas kernels  27.9 us (68%)
  starting transfers between devices  11.7 us (28%)
  between operations  1.54 us (4%)
    pallas_call x2, Pallas kernels, last(): pl.pallas_call(functools.partial(last_kernel, n, parts, to_image, PAIR_TI...  10.9 us
    pallas_call x1, Pallas kernels, own_tile(): pl.pallas_call(functools.partial(own_kernel, n), out_shape=(pltpu.VMEM((r...  8.79 us
    ppermute x2, starting transfers between devices, local(): near = [lax.ppermute(part, 'dp', near_pairs) for part in near_own]  8.6 us
    pallas_call x1, Pallas kernels, middle(): pl.pallas_call(functools.partial(middle_kernel, n), out_shape=pltpu.VMEM(...  4.83 us
    pallas_call x2, Pallas kernels, pick(): pl.pallas_call(functools.partial(pick_kernel, [(w[0], w[2]) for w in want...  3.36 us
    ppermute x2, starting transfers between devices, local(): far = [lax.ppermute(part, 'dp', far_pairs) for part in far_own]  3.11 us
  transfers between devices with their start and end apart: 4, of which 0 were waited for; matrix products, arithmetic and copies ran while one was open for 0% of the time, Pallas kernels for 55%

profile of v1, /device:TPU:1, one launch (start us, length us, event | category | flops | bytes accessed | tf_op | source)
XLA Modules:
  0.0 41.2 jit_solution(5989532680508725798)
XLA Ops:
  0.6 1.5 %shard_map.59.refs_1_.refs_0_ = bf16[768,1152]{1,0:T(8,128)(2,1)S(1)} custom-call(bf16[1024,1152]{1,0:T(8,128)(2,1)} %images_ref.3, bf16[1024,1152]{1,0:T(8,128)(2,1)} %texts_ref.3), custom_call_target="tpu_custom_call" | custom-call | bytes 3538944 | tf_op jit(solution)/shard_map/pallas_call | solution.py:96
  2.1 3.1 %collective-permute-start.1 = (bf16[768,1152]{1,0:T(8,128)(2,1)S(1)}, bf16[768,1152]{1,0:T(8,128)(2,1)S(1)}, u32[]{:S(2)}, u32[]{:S(2)}) collective-permute-start(bf16[768,1152]{1,0:T(8,128)(2,1)S(1)} %shard_map.59.refs_1_.refs_0_), channel_id=1, source_target_pairs={{0,255},{1,2},{2,1},{3,4},{4,3},{5,6},{6,5},{7,8},{8,7},{9,10},{10... | collective-permute-start | bytes 5308424 | tf_op jit(solution)/shard_map/ppermute | solution.py:276
  5.9 0.0 copy-start
  5.9 1.9 %shard_map.60 = (f32[8,1152]{1,0:T(8,128)S(1)}, bf16[256,1152]{1,0:T(8,128)(2,1)S(1)}, bf16[512,1152]{1,0:T(8,128)(2,1)S(1)}, bf16[512,1152]{1,0:T(8,128)(2,1)S(1)}) custom-call(bf16[1024,1152]{1,0:T(8,128)(2,1)} %images_ref.3, bf16[1024,1152]{1,0:T(8,128)(2,1)} %texts_ref.3, f32[1]{0:T(128)} %bitcast.2.refs_0_, bf16[768,1152]{1,0:T(8,128)(2,1)S(1)} %shard_map.59.refs_1_.refs_0_), custom_call_target="tpu_custom_call" | custom-call | bytes 5898240 | tf_op jit(solution)/shard_map/pallas_call | solution.py:96
  7.8 8.5 %collective-permute-start.2 = (bf16[512,1152]{1,0:T(8,128)(2,1)S(1)}, bf16[512,1152]{1,0:T(8,128)(2,1)S(1)}, u32[]{:S(2)}, u32[]{:S(2)}) collective-permute-start(bf16[512,1152]{1,0:T(8,128)(2,1)S(1)} %get-tuple-element.15.refs_2_.refs_0_), channel_id=1, source_target_pairs={{0,1},{1,0},{2,3},{3,2},{4,5},{5,4},{6,7},{7,6},{8,9},{9,8},{10,11... | collective-permute-start | bytes 3538952 | tf_op jit(solution)/shard_map/ppermute | solution.py:277
  16.3 0.1 collective-permute-start.3
  16.4 0.0 collective-permute-start
  16.4 0.0 copy-done
  16.4 8.8 %shard_map.61 = (f32[1024,1152]{1,0:T(8,128)S(1)}, f32[1024,1152]{1,0:T(8,128)S(1)}) custom-call(s32[1,1024]{1,0:T(1,128)S(1)} %bitcast.3, bf16[768,1152]{1,0:T(8,128)(2,1)S(1)} %shard_map.59.refs_1_.refs_0_, bf16[256,1152]{1,0:T(8,128)(2,1)S(1)} %get-tuple-element.14.refs_1_, bf16[512,1152]{1,0:T(8,128)(2,1)S(1)} %get-tuple-element.15.refs_2_.refs_0_, ...), custom_call_target="tpu_custom_call" | custom-call | flops 7247757312 | tf_op jit(solution)/shard_map/pallas_call | solution.py:154
  25.2 0.0 collective-permute-done.2.refs_2_
  25.2 0.0 collective-permute-done.3.refs_3_
  25.2 7.2 %shard_map.62 = (bf16[1024,1152]{1,0:T(8,128)(2,1)}, f32[1024,1152]{1,0:T(8,128)}) custom-call(bf16[512,1152]{1,0:T(8,128)(2,1)S(1)} %get-tuple-element.15.refs_2_.refs_0_, bf16[512,1152]{1,0:T(8,128)(2,1)S(1)} %get-tuple-element.16.refs_3_.refs_1_, bf16[512,1152]{1,0:T(8,128)(2,1)S(1)} %collective-permute-done.2.refs_2_, ...), custom_call_target="tpu_custom_call" | custom-call | flops 4831838208 | tf_op jit(solution)/shard_map/pallas_call | solution.py:219
  32.4 0.0 collective-permute-done.1.refs_2_
  32.4 4.8 %shard_map.63.refs_3_ = f32[1024,1152]{1,0:T(8,128)S(1)} custom-call(bf16[768,1152]{1,0:T(8,128)(2,1)S(1)} %shard_map.59.refs_1_.refs_0_, bf16[256,1152]{1,0:T(8,128)(2,1)S(1)} %get-tuple-element.14.refs_1_, bf16[768,1152]{1,0:T(8,128)(2,1)S(1)} %collective-permute-done.1.refs_2_, ...), custom_call_target="tpu_custom_call", output_to_operand_aliasing={{}: (3, {})} | custom-call | flops 3623878656 | tf_op jit(solution)/shard_map/pallas_call | solution.py:248
  37.3 0.0 collective-permute-done.refs_2_
  37.3 3.7 %shard_map.64 = (bf16[1024,1152]{1,0:T(8,128)(2,1)}, f32[1024,1152]{1,0:T(8,128)}) custom-call(bf16[768,1152]{1,0:T(8,128)(2,1)S(1)} %shard_map.59.refs_1_.refs_0_, bf16[256,1152]{1,0:T(8,128)(2,1)S(1)} %get-tuple-element.14.refs_1_, bf16[256,1152]{1,0:T(8,128)(2,1)S(1)} %collective-permute-done.refs_2_, ...), custom_call_target="tpu_custom_call", output_to_operand_aliasing={{0}: (5, {}), {1}: (6, {})} | custom-call | flops 1207959552 | tf_op jit(solution)/shard_map/pallas_call | solution.py:219
Async XLA Ops:
  2.1 30.3 %collective-permute-start.1 = (bf16[768,1152]{1,0:T(8,128)(2,1)S(1)}, bf16[768,1152]{1,0:T(8,128)(2,1)S(1)}, u32[]{:S(2)}, u32[]{:S(2)}) collective-permute-start(bf16[768,1152]{1,0:T(8,128)(2,1)S(1)} %shard_map.59.refs_1_.refs_0_), channel_id=1, source_target_pairs={{0,255},{1,2},{2,1},{3,4},{4,3},{5,6},{6,5},{7,8},{8,7},{9,10},{10... | collective-permute-start | bytes 5308424 | tf_op jit(solution)/shard_map/ppermute | solution.py:276
  5.9 10.5 %copy-start = (s32[1024]{0:T(1024)S(1)}, s32[1024]{0:T(1024)}, u32[]{:S(2)}) copy-start(s32[1024]{0:T(1024)} %param.6) | copy-start | bytes 12292
  7.8 17.4 %collective-permute-start.2 = (bf16[512,1152]{1,0:T(8,128)(2,1)S(1)}, bf16[512,1152]{1,0:T(8,128)(2,1)S(1)}, u32[]{:S(2)}, u32[]{:S(2)}) collective-permute-start(bf16[512,1152]{1,0:T(8,128)(2,1)S(1)} %get-tuple-element.15.refs_2_.refs_0_), channel_id=1, source_target_pairs={{0,1},{1,0},{2,3},{3,2},{4,5},{5,4},{6,7},{7,6},{8,9},{9,8},{10,11... | collective-permute-start | bytes 3538952 | tf_op jit(solution)/shard_map/ppermute | solution.py:277
  16.3 8.9 %collective-permute-start.3 = (bf16[512,1152]{1,0:T(8,128)(2,1)S(1)}, bf16[512,1152]{1,0:T(8,128)(2,1)S(1)}, u32[]{:S(2)}, u32[]{:S(2)}) collective-permute-start(bf16[512,1152]{1,0:T(8,128)(2,1)S(1)} %get-tuple-element.16.refs_3_.refs_1_), channel_id=1, source_target_pairs={{0,1},{1,0},{2,3},{3,2},{4,5},{5,4},{6,7},{7,6},{8,9},{9,8},{10,11... | collective-permute-start | bytes 3538952 | tf_op jit(solution)/shard_map/ppermute | solution.py:277
  16.4 20.9 %collective-permute-start = (bf16[256,1152]{1,0:T(8,128)(2,1)S(1)}, bf16[256,1152]{1,0:T(8,128)(2,1)S(1)}, u32[]{:S(2)}, u32[]{:S(2)}) collective-permute-start(bf16[256,1152]{1,0:T(8,128)(2,1)S(1)} %get-tuple-element.14.refs_1_), channel_id=1, source_target_pairs={{0,255},{1,2},{2,1},{3,4},{4,3},{5,6},{6,5},{7,8},{8,7},{9,10},{10... | collective-permute-start | bytes 1769480 | tf_op jit(solution)/shard_map/ppermute | solution.py:276

commit v2 on v1

v2 whole, which is shorter than its diff:
```python
import functools
import math

import jax
import jax.numpy as jnp
from jax import lax
from jax.experimental import pallas as pl
from jax.experimental.pallas import tpu as pltpu
from jax.sharding import PartitionSpec as P

LOGIT_SCALE = 10.0
SCORE_OFFSET = -2.0
FAR_ROWS = (768, 256)
NEAR_ROWS = (512, 512)
OWN_TILE = 256
HEAD_TILES = 2
LAST_TILE = 256
PICK_TILE = 128
PAIR_TILE = 512
NT = (((1,), (1,)), ((), ()))
NN = (((1,), (0,)), ((), ()))
TN = (((0,), (0,)), ((), ()))
VMEM = pl.BlockSpec(memory_space=pltpu.VMEM)
SMEM = pl.BlockSpec(memory_space=pltpu.SMEM)
ANY = pl.BlockSpec(memory_space=pl.ANY)


def mm(a, b, dims):
    return lax.dot_general(a, b, dims, preferred_element_type=jnp.float32)


def sigmoid(product):
    per_bit = 1.0 / math.log(2.0)
    return 1.0 / (1.0 + jnp.exp2(product * (-LOGIT_SCALE * per_bit) - SCORE_OFFSET * per_bit))


def in_vmem(x):
    return pltpu.with_memory_space_constraint(x, pltpu.VMEM)


def in_hbm(x):
    return pltpu.with_memory_space_constraint(x, pltpu.HBM)


def params(mib):
    return pltpu.CompilerParams(vmem_limit_bytes=mib << 20)


def cost(matmuls, rows, cols, depth):
    return pl.CostEstimate(flops=2 * matmuls * rows * cols * depth, bytes_accessed=0, transcendentals=0)


def is_even():
    return lax.rem(lax.axis_index("dp"), 2) == 0


def fetches(starts, images_ref, texts_ref, outs, sems):
    even = is_even()

    def copies(i, source):
        return [
            pltpu.make_async_copy(
                source.at[pl.ds(starts[i][0] + at, PICK_TILE), :], outs[i].at[pl.ds(at, PICK_TILE), :], sems.at[i, at // PICK_TILE]
            )
            for at in range(0, outs[i].shape[0], PICK_TILE)
        ]

    def begin(flipped):
        for i, (_, _, flip) in enumerate(starts):
            for copy in copies(i, images_ref if flip == flipped else texts_ref):
                copy.start()

    @pl.when(even)
    def _():
        begin(False)

    @pl.when(jnp.logical_not(even))
    def _():
        begin(True)

    def wait(i):
        for copy in copies(i, images_ref):
            copy.wait()

    return [functools.partial(wait, i) for i in range(len(starts))]


def semaphores(wanted):
    return pltpu.SemaphoreType.DMA((len(wanted), max(w[1] for w in wanted) // PICK_TILE))


def pick_kernel(wanted, images_ref, texts_ref, *refs):
    for wait in fetches(wanted, images_ref, texts_ref, refs[:-1], refs[-1]):
        wait()


def pick(images, texts, wanted):
    depth = images.shape[1]
    return pl.pallas_call(
        functools.partial(pick_kernel, wanted),
        out_shape=tuple(pltpu.VMEM((w[1], depth), images.dtype) for w in wanted),
        in_specs=[ANY] * 2,
        out_specs=(VMEM,) * len(wanted),
        scratch_shapes=[semaphores(wanted)],
        compiler_params=params(1),
    )(in_hbm(images), in_hbm(texts))


def across(coef, others):
    total, at = None, 0
    for other in others:
        part = mm(coef[:, at : at + other.shape[0]], other, NN)
        total = part if total is None else total + part
        at += other.shape[0]
    return total


def own_tiles(tiles, at, other_refs, match_ref, acc_a, acc_b):
    rows = acc_b.shape[0]
    even = is_even()
    first = lax.axis_index("dp") * rows
    match_row = match_ref[...] - first

    def load(t):
        ref, start = tiles[t]
        return ref[start : start + OWN_TILE, :]

    others = [ref[...] for ref in other_refs]

    def product_of(t):
        return jnp.concatenate([mm(load(t), other, NT) for other in others], axis=1)

    product = product_of(0)
    for t in range(len(tiles)):
        following = product_of(t + 1) if t + 1 < len(tiles) else None
        match_tile = jnp.broadcast_to(match_ref[:, at : at + OWN_TILE] - first, (128, OWN_TILE)).T
        match_col = jnp.concatenate([match_tile] * (rows // 128), axis=1)
        lane = lax.broadcasted_iota(jnp.int32, (OWN_TILE, rows), 1)
        row = lax.broadcasted_iota(jnp.int32, (OWN_TILE, rows), 0) + at
        gap = jnp.where(even, match_col - lane, match_row - row)
        coef = (sigmoid(product) - jnp.where(gap == 0, 1.0, 0.0)).astype(jnp.bfloat16)
        acc_a[at : at + OWN_TILE, :] = across(coef, others)
        term = mm(coef, load(t), TN)
        if at == 0:
            acc_b[...] = term
        else:
            acc_b[...] += term
        product = following
        at += OWN_TILE


def tiles_of(refs):
    return [(ref, start) for ref in refs for start in range(0, ref.shape[0], OWN_TILE)]


def head_kernel(wanted, bases, images_ref, texts_ref, match_ref, cotangent_ref, first_ref, *refs):
    *outs, acc_a, acc_b, scale_ref, sems = refs
    waits = fetches(wanted, images_ref, texts_ref, outs, sems)
    scale_ref[...] = jnp.full(scale_ref.shape, cotangent_ref[0] * (LOGIT_SCALE / acc_b.shape[0]), jnp.float32)
    tiles = tiles_of([first_ref])[:HEAD_TILES]
    for wait in waits[:bases]:
        wait()
    own_tiles(tiles, 0, outs[:bases], match_ref, acc_a, acc_b)
    for wait in waits[bases:]:
        wait()


def own_head(images, texts, match, cotangent, first, wanted, bases):
    rows, depth = images.shape
    return pl.pallas_call(
        functools.partial(head_kernel, wanted, bases),
        out_shape=(
            *(pltpu.VMEM((w[1], depth), images.dtype) for w in wanted),
            pltpu.VMEM((rows, depth), jnp.float32),
            pltpu.VMEM((rows, depth), jnp.float32),
            pltpu.VMEM((8, depth), jnp.float32),
        ),
        in_specs=[ANY, ANY, VMEM, SMEM, VMEM],
        out_specs=(VMEM,) * (len(wanted) + 3),
        scratch_shapes=[semaphores(wanted)],
        compiler_params=params(16),
        cost_estimate=cost(3, OWN_TILE * HEAD_TILES, rows, depth),
    )(in_hbm(images), in_hbm(texts), in_vmem(match), cotangent, in_vmem(first))


def rest_kernel(chunks, match_ref, *refs):
    a_refs, b_refs, (acc_a, acc_b) = refs[:chunks], refs[chunks:-4], refs[-2:]
    tiles = tiles_of(a_refs)[HEAD_TILES:]
    own_tiles(tiles, HEAD_TILES * OWN_TILE, b_refs, match_ref, acc_a, acc_b)


def own_rest(own, base, match, acc_a, acc_b):
    rows, depth = acc_a.shape
    n, given = len(own), 1 + len(own) + len(base)
    return pl.pallas_call(
        functools.partial(rest_kernel, n),
        out_shape=(pltpu.VMEM((rows, depth), jnp.float32), pltpu.VMEM((rows, depth), jnp.float32)),
        in_specs=[VMEM] * (given + 2),
        out_specs=(VMEM, VMEM),
        input_output_aliases={given: 0, given + 1: 1},
        compiler_params=params(16),
        cost_estimate=cost(3, rows - OWN_TILE * HEAD_TILES, rows, depth),
    )(in_vmem(match), *[in_vmem(o) for o in (*own, *base, acc_a, acc_b)])


def pair_tiles(own_refs, other_refs, tile):
    tiles = [(ref, start) for ref in own_refs for start in range(0, ref.shape[0], tile)]
    sizes = [min(tile, ref.shape[0] - start) for ref, start in tiles]
    others = [ref[...] for ref in other_refs]

    def products(t):
        ref, start = tiles[t]
        own = ref[start : start + sizes[t], :]
        return [mm(own, other, NT) for other in others]

    at, held = 0, products(0)
    for t in range(len(tiles)):
        following = products(t + 1) if t + 1 < len(tiles) else None
        term = None
        for product, other in zip(held, others, strict=True):
            part = mm(sigmoid(product).astype(jnp.bfloat16), other, NN)
            term = part if term is None else term + part
        yield t, at, sizes[t], term
        at += sizes[t]
        held = following


def near_kernel(chunks, *refs):
    own_refs, other_refs, rest = refs[:chunks], refs[chunks : 2 * chunks], refs[2 * chunks :]
    acc_ref, scale_ref, wide_ref, narrow_ref = rest

    def go(out_ref):
        scale = scale_ref[0:1, :]
        for _, at, size, term in pair_tiles(own_refs, other_refs, PAIR_TILE):
            rows = pl.ds(at, size)
            out_ref[rows, :] = (scale * (acc_ref[rows, :] + term)).astype(out_ref.dtype)

    @pl.when(is_even())
    def _():
        go(wide_ref)

    @pl.when(jnp.logical_not(is_even()))
    def _():
        go(narrow_ref)


def near_pair(own, other, acc, scale):
    rows, depth = acc.shape
    n = len(own)
    return pl.pallas_call(
        functools.partial(near_kernel, n),
        out_shape=(pltpu.VMEM((rows, depth), jnp.float32), pltpu.VMEM((rows, depth), jnp.bfloat16)),
        in_specs=[VMEM] * (2 * n + 2),
        out_specs=(VMEM, VMEM),
        input_output_aliases={2 * n: 0},
        compiler_params=params(16),
        cost_estimate=cost(2, rows, rows, depth),
    )(*[in_vmem(o) for o in (*own, *other, acc, scale)])


def last_kernel(chunks, tile, *refs):
    own_refs, other_ref, acc_ref, scale_ref = refs[:chunks], *refs[chunks : chunks + 3]
    image_ref, text_ref, wide, narrow, sems = refs[-5:]

    def go(stage, out_ref):
        scale = scale_ref[0:1, :]
        copies = []
        for t, at, size, term in pair_tiles(own_refs, [other_ref], tile):
            rows = pl.ds(at, size)
            stage[rows, :] = (scale * (acc_ref[rows, :] + term)).astype(stage.dtype)
            copies.append(pltpu.make_async_copy(stage.at[rows, :], out_ref.at[rows, :], sems.at[t]))
            copies[-1].start()
        for copy in copies:
            copy.wait()

    @pl.when(is_even())
    def _():
        go(narrow, image_ref)

    @pl.when(jnp.logical_not(is_even()))
    def _():
        go(wide, text_ref)


def last(own, other, acc, scale, outs, tile):
    rows, depth = acc.shape
    n = len(own)
    return pl.pallas_call(
        functools.partial(last_kernel, n, tile),
        out_shape=(
            jax.ShapeDtypeStruct((rows, depth), jnp.bfloat16),
            jax.ShapeDtypeStruct((rows, depth), jnp.float32),
        ),
        in_specs=[VMEM] * (n + 3) + [ANY] * 2,
        out_specs=(ANY, ANY),
        scratch_shapes=[
            pltpu.VMEM((rows, depth), jnp.float32),
            pltpu.VMEM((rows, depth), jnp.bfloat16),
            pltpu.SemaphoreType.DMA((rows // tile,)),
        ],
        input_output_aliases={n + 3 + i: i for i in range(2)},
        compiler_params=params(16),
        cost_estimate=cost(2, rows, other.shape[0], depth),
    )(*[in_vmem(o) for o in (*own, other, acc, scale)], *outs)


def middle_kernel(chunks, parts, *refs):
    own_refs, other_refs, rest = refs[:chunks], refs[chunks : chunks + parts], refs[chunks + parts :]
    acc_ref, wide_ref, narrow_ref, out_ref, image_ref, text_ref, sems = rest
    tile = acc_ref.shape[0] // sems.shape[0]

    def move(source, target, act):
        for i in range(sems.shape[0]):
            rows = pl.ds(i * tile, tile)
            act(pltpu.make_async_copy(source.at[rows, :], target.at[rows, :], sems.at[i]))

    def moves(act):
        @pl.when(is_even())
        def _():
            move(wide_ref, text_ref, act)

        @pl.when(jnp.logical_not(is_even()))
        def _():
            move(narrow_ref, image_ref, act)

    moves(lambda copy: copy.start())
    for _, at, size, term in pair_tiles(own_refs, other_refs, PAIR_TILE):
        rows = pl.ds(at, size)
        out_ref[rows, :] = acc_ref[rows, :] + term
    moves(lambda copy: copy.wait())


def middle(own, other, acc, done):
    rows, depth = acc.shape
    n, parts = len(own), len(other)
    return pl.pallas_call(
        functools.partial(middle_kernel, n, parts),
        out_shape=(
            pltpu.VMEM((rows, depth), jnp.float32),
            jax.ShapeDtypeStruct((rows, depth), jnp.bfloat16),
            jax.ShapeDtypeStruct((rows, depth), jnp.float32),
        ),
        in_specs=[VMEM] * (n + parts + 3),
        out_specs=(VMEM, ANY, ANY),
        scratch_shapes=[pltpu.SemaphoreType.DMA((4,))],
        input_output_aliases={n + parts: 0},
        compiler_params=params(16),
        cost_estimate=cost(2, rows, sum(o.shape[0] for o in other), depth),
    )(*[in_vmem(o) for o in (*own, *other, acc, *done)])


def spans(counts, flip):
    start = 0
    for count in counts:
        yield start, count, flip
        start += count


def local(images, texts, positive, loss_cotangent):
    rows = images.shape[0]
    size = lax.axis_size("dp")
    far_pairs = [(p, (p - 1) % size if p % 2 == 0 else (p + 1) % size) for p in range(size)]
    near_pairs = [(p, p + 1 if p % 2 == 0 else p - 1) for p in range(size)]
    match = positive.reshape(1, rows)
    (first,) = pick(images, texts, list(spans(FAR_ROWS, False))[:1])
    wanted = list(spans(NEAR_ROWS, True)) + list(spans(FAR_ROWS, False))[1:]
    bases = len(NEAR_ROWS)
    cotangent, first = lax.optimization_barrier((loss_cotangent, first))
    *picked, far_acc, near_acc, scale = own_head(images, texts, match, cotangent.reshape(1), first, wanted, bases)
    near_own, far_own = picked[:bases], [first, *picked[bases:]]
    far = [lax.ppermute(part, "dp", far_pairs) for part in far_own]
    near = [lax.ppermute(part, "dp", near_pairs) for part in near_own]
    far_acc, near_acc = own_rest(far_own, near_own, match, far_acc, near_acc)
    done = near_pair(near_own, near, near_acc, scale)
    far_acc, *outs = middle(far_own, far[:-1], far_acc, done)
    return last(far_own, far[-1], far_acc, scale, outs, LAST_TILE)


def solution(mesh):
    in_specs = (P("dp", None), P("dp", None), P("dp"), P())
    out_specs = (P("dp", None), P("dp", None))
    return jax.shard_map(local, mesh=mesh, in_specs=in_specs, out_specs=out_specs, check_vma=False)
```

time: 41.3 us -> 40 us (0.969)
  the two profiles are of different devices: /device:TPU:1 before, /device:TPU:0 now
where the time goes in v2:
time: 40 us; the launch traced here: 39.8 us
  Pallas kernels  27.6 us (69%)
  starting transfers between devices  9.6 us (24%)
  between operations  1.54 us (4%)
  waiting for transfers between devices  0.99 us (2%)
    ppermute x2, starting transfers between devices, local(): far = [lax.ppermute(part, 'dp', far_pairs) for part in far_own]  9.01 us
    pallas_call x1, Pallas kernels, near_pair(): pl.pallas_call(functools.partial(near_kernel, n), out_shape=(pltpu.VMEM((...  7.07 us
    pallas_call x1, Pallas kernels, own_head(): pl.pallas_call(functools.partial(head_kernel, wanted, bases), out_shape=(...  6.11 us
    pallas_call x1, Pallas kernels, middle(): pl.pallas_call(functools.partial(middle_kernel, n, parts), out_shape=(plt...  5.88 us
    pallas_call x1, Pallas kernels, own_rest(): pl.pallas_call(functools.partial(rest_kernel, n), out_shape=(pltpu.VMEM((...  4.45 us
    pallas_call x1, Pallas kernels, last(): pl.pallas_call(functools.partial(last_kernel, n, tile), out_shape=(jax.Sh...  2.66 us
    pallas_call x1, Pallas kernels, pick(): pl.pallas_call(functools.partial(pick_kernel, wanted), out_shape=tuple((p...  1.47 us
    ppermute x2, waiting for transfers between devices, local(): far = [lax.ppermute(part, 'dp', far_pairs) for part in far_own]  0.99 us
  transfers between devices with their start and end apart: 4, of which 2 were waited for; matrix products, arithmetic and copies ran while one was open for 0% of the time, Pallas kernels for 59%

profile of v2, /device:TPU:0, one launch (start us, length us, event | category | flops | bytes accessed | tf_op | source)
XLA Modules:
  0.0 39.8 jit_solution(3348943516504404632)
XLA Ops:
  0.6 0.0 copy-start
  0.6 1.5 %shard_map.59.first_ref.refs_0_ = bf16[768,1152]{1,0:T(8,128)(2,1)S(1)} custom-call(bf16[1024,1152]{1,0:T(8,128)(2,1)} %images_ref.3, bf16[1024,1152]{1,0:T(8,128)(2,1)} %texts_ref.3), custom_call_target="tpu_custom_call" | custom-call | tf_op jit(solution)/shard_map/pallas_call | solution.py:99
  2.1 8.3 %collective-permute-start.1 = (bf16[768,1152]{1,0:T(8,128)(2,1)S(1)}, bf16[768,1152]{1,0:T(8,128)(2,1)S(1)}, u32[]{:S(2)}, u32[]{:S(2)}) collective-permute-start(bf16[768,1152]{1,0:T(8,128)(2,1)S(1)} %shard_map.59.first_ref.refs_0_), channel_id=1, source_target_pairs={{0,255},{1,2},{2,1},{3,4},{4,3},{5,6},{6,5},{7,8},{8,7},{9,10},{10... | collective-permute-start | bytes 5308424 | tf_op jit(solution)/shard_map/ppermute | solution.py:371
  11.1 0.0 copy-done
  11.1 6.1 %shard_map.60 = (bf16[512,1152]{1,0:T(8,128)(2,1)S(1)}, bf16[512,1152]{1,0:T(8,128)(2,1)S(1)}, bf16[256,1152]{1,0:T(8,128)(2,1)S(1)}, f32[1024,1152]{1,0:T(8,128...) custom-call(bf16[1024,1152]{1,0:T(8,128)(2,1)} %images_ref.3, bf16[1024,1152]{1,0:T(8,128)(2,1)} %texts_ref.3, ...), custom_call_target="tpu_custom_call" | custom-call | flops 3623878656 | tf_op jit(solution)/shard_map/pallas_call | solution.py:170
  17.2 0.1 collective-permute-start.2
  17.3 0.5 %collective-permute-start.3 = (bf16[512,1152]{1,0:T(8,128)(2,1)S(1)}, bf16[512,1152]{1,0:T(8,128)(2,1)S(1)}, u32[]{:S(2)}, u32[]{:S(2)}) collective-permute-start(bf16[512,1152]{1,0:T(8,128)(2,1)S(1)} %get-tuple-element.21.refs_3_.refs_1_), channel_id=1, source_target_pairs={{0,1},{1,0},{2,3},{3,2},{4,5},{5,4},{6,7},{7,6},{8,9},{9,8},{10,11... | collective-permute-start | bytes 3538952 | tf_op jit(solution)/shard_map/ppermute | solution.py:372
  17.8 0.7 %collective-permute-start = (bf16[256,1152]{1,0:T(8,128)(2,1)S(1)}, bf16[256,1152]{1,0:T(8,128)(2,1)S(1)}, u32[]{:S(2)}, u32[]{:S(2)}) collective-permute-start(bf16[256,1152]{1,0:T(8,128)(2,1)S(1)} %get-tuple-element.19.refs_1_), channel_id=1, source_target_pairs={{0,255},{1,2},{2,1},{3,4},{4,3},{5,6},{6,5},{7,8},{8,7},{9,10},{10... | collective-permute-start | bytes 1769480 | tf_op jit(solution)/shard_map/ppermute | solution.py:371
  18.5 4.5 %shard_map.61 = (f32[1024,1152]{1,0:T(8,128)S(1)}, f32[1024,1152]{1,0:T(8,128)S(1)}) custom-call(s32[1,1024]{1,0:T(1,128)S(1)} %bitcast.4, bf16[768,1152]{1,0:T(8,128)(2,1)S(1)} %shard_map.59.first_ref.refs_0_, bf16[256,1152]{1,0:T(8,128)(2,1)S(1)} %get-tuple-element.19.refs_1_, ...), custom_call_target="tpu_custom_call", output_to_operand_aliasing={{0}: (5, {}), {1}: (6, {})} | custom-call | flops 3623878656 | tf_op jit(solution)/shard_map/pallas_call | solution.py:195
  23.0 0.0 collective-permute-done.2.refs_2_
  23.0 0.0 collective-permute-done.3.refs_3_
  23.0 7.1 %shard_map.62 = (f32[1024,1152]{1,0:T(8,128)S(1)}, bf16[1024,1152]{1,0:T(8,128)(2,1)S(1)}) custom-call(bf16[512,1152]{1,0:T(8,128)(2,1)S(1)} %get-tuple-element.20.refs_2_.refs_0_, bf16[512,1152]{1,0:T(8,128)(2,1)S(1)} %get-tuple-element.21.refs_3_.refs_1_, bf16[512,1152]{1,0:T(8,128)(2,1)S(1)} %collective-permute-done.2.refs_2_, ...), custom_call_target="tpu_custom_call", output_to_operand_aliasing={{0}: (4, {})} | custom-call | flops 4831838208 | tf_op jit(solution)/shard_map/pallas_call | solution.py:250
  30.1 0.6 %collective-permute-done.1.refs_2_ = bf16[768,1152]{1,0:T(8,128)(2,1)S(1)} collective-permute-done((bf16[768,1152]{1,0:T(8,128)(2,1)S(1)}, bf16[768,1152]{1,0:T(8,128)(2,1)S(1)}, u32[]{:S(2)}, u32[]{:S(2)}) %collective-permute-start.1) | collective-permute-done | bytes 1769504 | tf_op jit(solution)/shard_map/ppermute | solution.py:371
  30.6 5.9 %shard_map.63 = (f32[1024,1152]{1,0:T(8,128)S(1)}, bf16[1024,1152]{1,0:T(8,128)(2,1)}, f32[1024,1152]{1,0:T(8,128)}) custom-call(bf16[768,1152]{1,0:T(8,128)(2,1)S(1)} %shard_map.59.first_ref.refs_0_, bf16[256,1152]{1,0:T(8,128)(2,1)S(1)} %get-tuple-element.19.refs_1_, ...), custom_call_target="tpu_custom_call", output_to_operand_aliasing={{0}: (3, {})} | custom-call | flops 3623878656 | tf_op jit(solution)/shard_map/pallas_call | solution.py:336
  36.5 0.4 %collective-permute-done.refs_2_ = bf16[256,1152]{1,0:T(8,128)(2,1)S(1)} collective-permute-done((bf16[256,1152]{1,0:T(8,128)(2,1)S(1)}, bf16[256,1152]{1,0:T(8,128)(2,1)S(1)}, u32[]{:S(2)}, u32[]{:S(2)}) %collective-permute-start) | collective-permute-done | bytes 589856 | tf_op jit(solution)/shard_map/ppermute | solution.py:371
  36.9 2.7 %shard_map.64 = (bf16[1024,1152]{1,0:T(8,128)(2,1)}, f32[1024,1152]{1,0:T(8,128)}) custom-call(bf16[768,1152]{1,0:T(8,128)(2,1)S(1)} %shard_map.59.first_ref.refs_0_, bf16[256,1152]{1,0:T(8,128)(2,1)S(1)} %get-tuple-element.19.refs_1_, bf16[256,1152]{1,0:T(8,128)(2,1)S(1)} %collective-permute-done.refs_2_, ...), custom_call_target="tpu_custom_call", output_to_operand_aliasing={{0}: (5, {}), {1}: (6, {})} | custom-call | flops 1207959552 | tf_op jit(solution)/shard_map/pallas_call | solution.py:288
Async XLA Ops:
  0.6 10.4 %copy-start = (s32[1024]{0:T(1024)S(1)}, s32[1024]{0:T(1024)}, u32[]{:S(2)}) copy-start(s32[1024]{0:T(1024)} %param.6) | copy-start | bytes 12292
  2.1 28.5 %collective-permute-start.1 = (bf16[768,1152]{1,0:T(8,128)(2,1)S(1)}, bf16[768,1152]{1,0:T(8,128)(2,1)S(1)}, u32[]{:S(2)}, u32[]{:S(2)}) collective-permute-start(bf16[768,1152]{1,0:T(8,128)(2,1)S(1)} %shard_map.59.first_ref.refs_0_), channel_id=1, source_target_pairs={{0,255},{1,2},{2,1},{3,4},{4,3},{5,6},{6,5},{7,8},{8,7},{9,10},{10... | collective-permute-start | bytes 5308424 | tf_op jit(solution)/shard_map/ppermute | solution.py:371
  17.2 5.8 %collective-permute-start.2 = (bf16[512,1152]{1,0:T(8,128)(2,1)S(1)}, bf16[512,1152]{1,0:T(8,128)(2,1)S(1)}, u32[]{:S(2)}, u32[]{:S(2)}) collective-permute-start(bf16[512,1152]{1,0:T(8,128)(2,1)S(1)} %get-tuple-element.20.refs_2_.refs_0_), channel_id=1, source_target_pairs={{0,1},{1,0},{2,3},{3,2},{4,5},{5,4},{6,7},{7,6},{8,9},{9,8},{10,11... | collective-permute-start | bytes 3538952 | tf_op jit(solution)/shard_map/ppermute | solution.py:372
  17.3 5.7 %collective-permute-start.3 = (bf16[512,1152]{1,0:T(8,128)(2,1)S(1)}, bf16[512,1152]{1,0:T(8,128)(2,1)S(1)}, u32[]{:S(2)}, u32[]{:S(2)}) collective-permute-start(bf16[512,1152]{1,0:T(8,128)(2,1)S(1)} %get-tuple-element.21.refs_3_.refs_1_), channel_id=1, source_target_pairs={{0,1},{1,0},{2,3},{3,2},{4,5},{5,4},{6,7},{7,6},{8,9},{9,8},{10,11... | collective-permute-start | bytes 3538952 | tf_op jit(solution)/shard_map/ppermute | solution.py:372
  17.8 19.2 %collective-permute-start = (bf16[256,1152]{1,0:T(8,128)(2,1)S(1)}, bf16[256,1152]{1,0:T(8,128)(2,1)S(1)}, u32[]{:S(2)}, u32[]{:S(2)}) collective-permute-start(bf16[256,1152]{1,0:T(8,128)(2,1)S(1)} %get-tuple-element.19.refs_1_), channel_id=1, source_target_pairs={{0,255},{1,2},{2,1},{3,4},{4,3},{5,6},{6,5},{7,8},{8,7},{9,10},{10... | collective-permute-start | bytes 1769480 | tf_op jit(solution)/shard_map/ppermute | solution.py:371

commit v3 on v2

--- a/solution.py
+++ b/solution.py
@@ -13,7 +13,8 @@
 FAR_ROWS = (768, 256)
 NEAR_ROWS = (512, 512)
 OWN_TILE = 256
-HEAD_TILES = 2
+EVEN_HEAD = 1
+ODD_HEAD = 2
 LAST_TILE = 256
 PICK_TILE = 128
 PAIR_TILE = 512
@@ -157,10 +158,15 @@
     *outs, acc_a, acc_b, scale_ref, sems = refs
     waits = fetches(wanted, images_ref, texts_ref, outs, sems)
     scale_ref[...] = jnp.full(scale_ref.shape, cotangent_ref[0] * (LOGIT_SCALE / acc_b.shape[0]), jnp.float32)
-    tiles = tiles_of([first_ref])[:HEAD_TILES]
+    tiles = tiles_of([first_ref])
     for wait in waits[:bases]:
         wait()
-    own_tiles(tiles, 0, outs[:bases], match_ref, acc_a, acc_b)
+    own_tiles(tiles[:EVEN_HEAD], 0, outs[:bases], match_ref, acc_a, acc_b)
+
+    @pl.when(jnp.logical_not(is_even()))
+    def _():
+        own_tiles(tiles[EVEN_HEAD:ODD_HEAD], EVEN_HEAD * OWN_TILE, outs[:bases], match_ref, acc_a, acc_b)
+
     for wait in waits[bases:]:
         wait()
 
@@ -179,14 +185,14 @@
         out_specs=(VMEM,) * (len(wanted) + 3),
         scratch_shapes=[semaphores(wanted)],
         compiler_params=params(16),
-        cost_estimate=cost(3, OWN_TILE * HEAD_TILES, rows, depth),
+        cost_estimate=cost(3, OWN_TILE * ODD_HEAD, rows, depth),
     )(in_hbm(images), in_hbm(texts), in_vmem(match), cotangent, in_vmem(first))
 
 
 def rest_kernel(chunks, match_ref, *refs):
     a_refs, b_refs, (acc_a, acc_b) = refs[:chunks], refs[chunks:-4], refs[-2:]
-    tiles = tiles_of(a_refs)[HEAD_TILES:]
-    own_tiles(tiles, HEAD_TILES * OWN_TILE, b_refs, match_ref, acc_a, acc_b)
+    tiles = tiles_of(a_refs)[ODD_HEAD:]
+    own_tiles(tiles, ODD_HEAD * OWN_TILE, b_refs, match_ref, acc_a, acc_b)
 
 
 def own_rest(own, base, match, acc_a, acc_b):
@@ -199,8 +205,35 @@
         out_specs=(VMEM, VMEM),
         input_output_aliases={given: 0, given + 1: 1},
         compiler_params=params(16),
-        cost_estimate=cost(3, rows - OWN_TILE * HEAD_TILES, rows, depth),
+        cost_estimate=cost(3, rows - OWN_TILE * ODD_HEAD, rows, depth),
     )(in_vmem(match), *[in_vmem(o) for o in (*own, *base, acc_a, acc_b)])
+
+
+def catch_up_kernel(match_ref, first_ref, later_ref, *refs):
+    b_refs, (acc_a, acc_b) = refs[:-5], refs[-2:]
+    tiles = tiles_of([first_ref])[EVEN_HEAD:ODD_HEAD]
+
+    @pl.when(is_even())
+    def _():
+        own_tiles(tiles, EVEN_HEAD * OWN_TILE, b_refs, match_ref, acc_a, acc_b)
+
+
+def catch_up(first, later, base, match, acc_a, acc_b):
+    rows, depth = acc_a.shape
+    given = 3 + len(base)
+    return pl.pallas_call(
+        catch_up_kernel,
+        out_shape=(
+            pltpu.VMEM(later.shape, later.dtype),
+            pltpu.VMEM((rows, depth), jnp.float32),
+            pltpu.VMEM((rows, depth), jnp.float32),
+        ),
+        in_specs=[VMEM] * (given + 2),
+        out_specs=(VMEM,) * 3,
+        input_output_aliases={2: 0, given: 1, given + 1: 2},
+        compiler_params=params(16),
+        cost_estimate=cost(3, OWN_TILE * (ODD_HEAD - EVEN_HEAD), rows, depth),
+    )(in_vmem(match), *[in_vmem(o) for o in (first, later, *base, acc_a, acc_b)])
 
 
 def pair_tiles(own_refs, other_refs, tile):
@@ -367,7 +400,9 @@
     bases = len(NEAR_ROWS)
     cotangent, first = lax.optimization_barrier((loss_cotangent, first))
     *picked, far_acc, near_acc, scale = own_head(images, texts, match, cotangent.reshape(1), first, wanted, bases)
-    near_own, far_own = picked[:bases], [first, *picked[bases:]]
+    near_own = picked[:bases]
+    later, far_acc, near_acc = catch_up(first, picked[bases], near_own, match, far_acc, near_acc)
+    far_own = [first, later]
     far = [lax.ppermute(part, "dp", far_pairs) for part in far_own]
     near = [lax.ppermute(part, "dp", near_pairs) for part in near_own]
     far_acc, near_acc = own_rest(far_own, near_own, match, far_acc, near_acc)

time: 40 us -> 39.9 us (level)
  starting transfers between devices: 9.6 us -> 9.16 us
    pallas_call x0 -> x1, Pallas kernels: none -> 2.46 us  [catch_up(): pl.pallas_call(catch_up_kernel, out_shape=(pltpu.VMEM(later.shape, later....]
    pallas_call x1, Pallas kernels: 6.11 us -> 4.23 us  [own_head(): pl.pallas_call(functools.partial(head_kernel, wanted, bases), out_shape=(...]
    ppermute x2, starting transfers between devices: 9.01 us -> 8.57 us  [local(): far = [lax.ppermute(part, 'dp', far_pairs) for part in far_own]]
  transfers between devices with their start and end apart: 4 -> 4, of which waited for: 2 -> 2; matrix products, arithmetic and copies ran while one was open for 0% -> 0% of each run, Pallas kernels for 59% -> 60%
where the time goes in v3:
time: 39.9 us; the launch traced here: 39.8 us
  Pallas kernels  28 us (70%)
  starting transfers between devices  9.16 us (23%)
  between operations  1.56 us (4%)
  waiting for transfers between devices  1.02 us (3%)
    ppermute x2, starting transfers between devices, local(): far = [lax.ppermute(part, 'dp', far_pairs) for part in far_own]  8.57 us
    pallas_call x1, Pallas kernels, near_pair(): pl.pallas_call(functools.partial(near_kernel, n), out_shape=(pltpu.VMEM((...  6.89 us
    pallas_call x1, Pallas kernels, middle(): pl.pallas_call(functools.partial(middle_kernel, n, parts), out_shape=(plt...  5.88 us
    pallas_call x1, Pallas kernels, own_rest(): pl.pallas_call(functools.partial(rest_kernel, n), out_shape=(pltpu.VMEM((...  4.45 us
    pallas_call x1, Pallas kernels, own_head(): pl.pallas_call(functools.partial(head_kernel, wanted, bases), out_shape=(...  4.23 us
    pallas_call x1, Pallas kernels, last(): pl.pallas_call(functools.partial(last_kernel, n, tile), out_shape=(jax.Sh...  2.66 us
    pallas_call x1, Pallas kernels, catch_up(): pl.pallas_call(catch_up_kernel, out_shape=(pltpu.VMEM(later.shape, later....  2.46 us
    pallas_call x1, Pallas kernels, pick(): pl.pallas_call(functools.partial(pick_kernel, wanted), out_shape=tuple((p...  1.47 us
  transfers between devices with their start and end apart: 4, of which 2 were waited for; matrix products, arithmetic and copies ran while one was open for 0% of the time, Pallas kernels for 60%

profile of v3, /device:TPU:0, one launch (start us, length us, event | category | flops | bytes accessed | tf_op | source)
XLA Modules:
  0.0 39.8 jit_solution(515782976546615193)
XLA Ops:
  0.6 0.0 copy-start
  0.6 1.5 %shard_map.59.first_ref.refs_0_ = bf16[768,1152]{1,0:T(8,128)(2,1)S(1)} custom-call(bf16[1024,1152]{1,0:T(8,128)(2,1)} %images_ref.3, bf16[1024,1152]{1,0:T(8,128)(2,1)} %texts_ref.3), custom_call_target="tpu_custom_call" | custom-call | tf_op jit(solution)/shard_map/pallas_call | solution.py:100
  2.1 8.3 %collective-permute-start.1 = (bf16[768,1152]{1,0:T(8,128)(2,1)S(1)}, bf16[768,1152]{1,0:T(8,128)(2,1)S(1)}, u32[]{:S(2)}, u32[]{:S(2)}) collective-permute-start(bf16[768,1152]{1,0:T(8,128)(2,1)S(1)} %shard_map.59.first_ref.refs_0_), channel_id=1, source_target_pairs={{0,255},{1,2},{2,1},{3,4},{4,3},{5,6},{6,5},{7,8},{8,7},{9,10},{10... | collective-permute-start | bytes 5308424 | tf_op jit(solution)/shard_map/ppermute | solution.py:406
  11.1 0.0 copy-done
  11.1 4.2 %shard_map.60 = (bf16[512,1152]{1,0:T(8,128)(2,1)S(1)}, bf16[512,1152]{1,0:T(8,128)(2,1)S(1)}, bf16[256,1152]{1,0:T(8,128)(2,1)S(1)}, f32[1024,1152]{1,0:T(8,128...) custom-call(bf16[1024,1152]{1,0:T(8,128)(2,1)} %images_ref.3, bf16[1024,1152]{1,0:T(8,128)(2,1)} %texts_ref.3, ...), custom_call_target="tpu_custom_call" | custom-call | flops 3623878656 | tf_op jit(solution)/shard_map/pallas_call | solution.py:176
  15.3 0.1 collective-permute-start.2
  15.4 0.5 %collective-permute-start.3 = (bf16[512,1152]{1,0:T(8,128)(2,1)S(1)}, bf16[512,1152]{1,0:T(8,128)(2,1)S(1)}, u32[]{:S(2)}, u32[]{:S(2)}) collective-permute-start(bf16[512,1152]{1,0:T(8,128)(2,1)S(1)} %get-tuple-element.24.refs_1_.refs_3_), channel_id=1, source_target_pairs={{0,1},{1,0},{2,3},{3,2},{4,5},{5,4},{6,7},{7,6},{8,9},{9,8},{10,11... | collective-permute-start | bytes 3538952 | tf_op jit(solution)/shard_map/ppermute | solution.py:407
  15.9 2.5 %shard_map.61 = (bf16[256,1152]{1,0:T(8,128)(2,1)S(1)}, f32[1024,1152]{1,0:T(8,128)S(1)}, f32[1024,1152]{1,0:T(8,128)S(1)}) custom-call(s32[1,1024]{1,0:T(1,128)S(1)} %bitcast.4, bf16[768,1152]{1,0:T(8,128)(2,1)S(1)} %shard_map.59.first_ref.refs_0_, ...), custom_call_target="tpu_custom_call", output_to_operand_aliasing={{0}: (2, {}), {1}: (5, {}), {2}: (6, {})} | custom-call | flops 1811939328 | tf_op jit(solution)/shard_map/pallas_call | solution.py:224
  18.4 0.3 collective-permute-start
  18.7 4.5 %shard_map.62 = (f32[1024,1152]{1,0:T(8,128)S(1)}, f32[1024,1152]{1,0:T(8,128)S(1)}) custom-call(s32[1,1024]{1,0:T(1,128)S(1)} %bitcast.5, bf16[768,1152]{1,0:T(8,128)(2,1)S(1)} %shard_map.59.first_ref.refs_0_, bf16[256,1152]{1,0:T(8,128)(2,1)S(1)} %get-tuple-element.27.refs_1_, ...), custom_call_target="tpu_custom_call", output_to_operand_aliasing={{0}: (5, {}), {1}: (6, {})} | custom-call | flops 3623878656 | tf_op jit(solution)/shard_map/pallas_call | solution.py:201
  23.1 0.0 collective-permute-done.2.refs_2_
  23.1 0.0 collective-permute-done.3.refs_3_
  23.1 6.9 %shard_map.63 = (f32[1024,1152]{1,0:T(8,128)S(1)}, bf16[1024,1152]{1,0:T(8,128)(2,1)S(1)}) custom-call(bf16[512,1152]{1,0:T(8,128)(2,1)S(1)} %get-tuple-element.23.refs_0_.refs_2_, bf16[512,1152]{1,0:T(8,128)(2,1)S(1)} %get-tuple-element.24.refs_1_.refs_3_, bf16[512,1152]{1,0:T(8,128)(2,1)S(1)} %collective-permute-done.2.refs_2_, ...), custom_call_target="tpu_custom_call", output_to_operand_aliasing={{0}: (4, {})} | custom-call | flops 4831838208 | tf_op jit(solution)/shard_map/pallas_call | solution.py:283
  30.0 0.6 %collective-permute-done.1.refs_2_ = bf16[768,1152]{1,0:T(8,128)(2,1)S(1)} collective-permute-done((bf16[768,1152]{1,0:T(8,128)(2,1)S(1)}, bf16[768,1152]{1,0:T(8,128)(2,1)S(1)}, u32[]{:S(2)}, u32[]{:S(2)}) %collective-permute-start.1) | collective-permute-done | bytes 1769504 | tf_op jit(solution)/shard_map/ppermute | solution.py:406
  30.6 5.9 %shard_map.64 = (f32[1024,1152]{1,0:T(8,128)S(1)}, bf16[1024,1152]{1,0:T(8,128)(2,1)}, f32[1024,1152]{1,0:T(8,128)}) custom-call(bf16[768,1152]{1,0:T(8,128)(2,1)S(1)} %shard_map.59.first_ref.refs_0_, bf16[256,1152]{1,0:T(8,128)(2,1)S(1)} %get-tuple-element.27.refs_1_, ...), custom_call_target="tpu_custom_call", output_to_operand_aliasing={{0}: (3, {})} | custom-call | flops 3623878656 | tf_op jit(solution)/shard_map/pallas_call | solution.py:369
  36.5 0.4 %collective-permute-done.refs_2_ = bf16[256,1152]{1,0:T(8,128)(2,1)S(1)} collective-permute-done((bf16[256,1152]{1,0:T(8,128)(2,1)S(1)}, bf16[256,1152]{1,0:T(8,128)(2,1)S(1)}, u32[]{:S(2)}, u32[]{:S(2)}) %collective-permute-start) | collective-permute-done | bytes 589856 | tf_op jit(solution)/shard_map/ppermute | solution.py:406
  36.9 2.7 %shard_map.65 = (bf16[1024,1152]{1,0:T(8,128)(2,1)}, f32[1024,1152]{1,0:T(8,128)}) custom-call(bf16[768,1152]{1,0:T(8,128)(2,1)S(1)} %shard_map.59.first_ref.refs_0_, bf16[256,1152]{1,0:T(8,128)(2,1)S(1)} %get-tuple-element.27.refs_1_, bf16[256,1152]{1,0:T(8,128)(2,1)S(1)} %collective-permute-done.refs_2_, ...), custom_call_target="tpu_custom_call", output_to_operand_aliasing={{0}: (5, {}), {1}: (6, {})} | custom-call | flops 1207959552 | tf_op jit(solution)/shard_map/pallas_call | solution.py:321
Async XLA Ops:
  0.6 10.4 %copy-start = (s32[1024]{0:T(1024)S(1)}, s32[1024]{0:T(1024)}, u32[]{:S(2)}) copy-start(s32[1024]{0:T(1024)} %param.6) | copy-start | bytes 12292
  2.1 28.5 %collective-permute-start.1 = (bf16[768,1152]{1,0:T(8,128)(2,1)S(1)}, bf16[768,1152]{1,0:T(8,128)(2,1)S(1)}, u32[]{:S(2)}, u32[]{:S(2)}) collective-permute-start(bf16[768,1152]{1,0:T(8,128)(2,1)S(1)} %shard_map.59.first_ref.refs_0_), channel_id=1, source_target_pairs={{0,255},{1,2},{2,1},{3,4},{4,3},{5,6},{6,5},{7,8},{8,7},{9,10},{10... | collective-permute-start | bytes 5308424 | tf_op jit(solution)/shard_map/ppermute | solution.py:406
  15.3 7.8 %collective-permute-start.2 = (bf16[512,1152]{1,0:T(8,128)(2,1)S(1)}, bf16[512,1152]{1,0:T(8,128)(2,1)S(1)}, u32[]{:S(2)}, u32[]{:S(2)}) collective-permute-start(bf16[512,1152]{1,0:T(8,128)(2,1)S(1)} %get-tuple-element.23.refs_0_.refs_2_), channel_id=1, source_target_pairs={{0,1},{1,0},{2,3},{3,2},{4,5},{5,4},{6,7},{7,6},{8,9},{9,8},{10,11... | collective-permute-start | bytes 3538952 | tf_op jit(solution)/shard_map/ppermute | solution.py:407
  15.4 7.7 %collective-permute-start.3 = (bf16[512,1152]{1,0:T(8,128)(2,1)S(1)}, bf16[512,1152]{1,0:T(8,128)(2,1)S(1)}, u32[]{:S(2)}, u32[]{:S(2)}) collective-permute-start(bf16[512,1152]{1,0:T(8,128)(2,1)S(1)} %get-tuple-element.24.refs_1_.refs_3_), channel_id=1, source_target_pairs={{0,1},{1,0},{2,3},{3,2},{4,5},{5,4},{6,7},{7,6},{8,9},{9,8},{10,11... | collective-permute-start | bytes 3538952 | tf_op jit(solution)/shard_map/ppermute | solution.py:407
  18.4 18.6 %collective-permute-start = (bf16[256,1152]{1,0:T(8,128)(2,1)S(1)}, bf16[256,1152]{1,0:T(8,128)(2,1)S(1)}, u32[]{:S(2)}, u32[]{:S(2)}) collective-permute-start(bf16[256,1152]{1,0:T(8,128)(2,1)S(1)} %get-tuple-element.27.refs_1_), channel_id=1, source_target_pairs={{0,255},{1,2},{2,1},{3,4},{4,3},{5,6},{6,5},{7,8},{8,7},{9,10},{10... | collective-permute-start | bytes 1769480 | tf_op jit(solution)/shard_map/ppermute | solution.py:406

commit v4 on v3

--- a/solution.py
+++ b/solution.py
@@ -285,7 +285,6 @@
         out_shape=(pltpu.VMEM((rows, depth), jnp.float32), pltpu.VMEM((rows, depth), jnp.bfloat16)),
         in_specs=[VMEM] * (2 * n + 2),
         out_specs=(VMEM, VMEM),
-        input_output_aliases={2 * n: 0},
         compiler_params=params(16),
         cost_estimate=cost(2, rows, rows, depth),
     )(*[in_vmem(o) for o in (*own, *other, acc, scale)])

time: 39.9 us -> 40 us (level)
  waiting for transfers between devices: 1.02 us -> 1.63 us
  Pallas kernels: 28 us -> 27.5 us
    pallas_call x1, Pallas kernels: 6.89 us -> 6.2 us  [near_pair(): pl.pallas_call(functools.partial(near_kernel, n), out_shape=(pltpu.VMEM((...]
    ppermute x2, waiting for transfers between devices: 1.01 us -> 1.62 us  [local(): far = [lax.ppermute(part, 'dp', far_pairs) for part in far_own]]
  transfers between devices with their start and end apart: 4 -> 4, of which waited for: 2 -> 2; matrix products, arithmetic and copies ran while one was open for 0% -> 0% of each run, Pallas kernels for 60% -> 59%
where the time goes in v4:
time: 40 us; the launch traced here: 39.8 us
  Pallas kernels  27.5 us (69%)
  starting transfers between devices  9.16 us (23%)
  waiting for transfers between devices  1.63 us (4%)
  between operations  1.56 us (4%)
    ppermute x2, starting transfers between devices, local(): far = [lax.ppermute(part, 'dp', far_pairs) for part in far_own]  8.57 us
    pallas_call x1, Pallas kernels, near_pair(): pl.pallas_call(functools.partial(near_kernel, n), out_shape=(pltpu.VMEM((...  6.2 us
    pallas_call x1, Pallas kernels, middle(): pl.pallas_call(functools.partial(middle_kernel, n, parts), out_shape=(plt...  5.89 us
    pallas_call x1, Pallas kernels, own_rest(): pl.pallas_call(functools.partial(rest_kernel, n), out_shape=(pltpu.VMEM((...  4.5 us
    pallas_call x1, Pallas kernels, own_head(): pl.pallas_call(functools.partial(head_kernel, wanted, bases), out_shape=(...  4.23 us
    pallas_call x1, Pallas kernels, last(): pl.pallas_call(functools.partial(last_kernel, n, tile), out_shape=(jax.Sh...  2.71 us
    pallas_call x1, Pallas kernels, catch_up(): pl.pallas_call(catch_up_kernel, out_shape=(pltpu.VMEM(later.shape, later....  2.48 us
    ppermute x2, waiting for transfers between devices, local(): far = [lax.ppermute(part, 'dp', far_pairs) for part in far_own]  1.62 us
  transfers between devices with their start and end apart: 4, of which 2 were waited for; matrix products, arithmetic and copies ran while one was open for 0% of the time, Pallas kernels for 59%

profile of v4, /device:TPU:0, one launch (start us, length us, event | category | flops | bytes accessed | tf_op | source)
XLA Modules:
  0.0 39.8 jit_solution(7073972869948276643)
XLA Ops:
  0.6 0.0 copy-start
  0.6 1.5 %shard_map.59.first_ref.refs_0_ = bf16[768,1152]{1,0:T(8,128)(2,1)S(1)} custom-call(bf16[1024,1152]{1,0:T(8,128)(2,1)} %images_ref.3, bf16[1024,1152]{1,0:T(8,128)(2,1)} %texts_ref.3), custom_call_target="tpu_custom_call" | custom-call | tf_op jit(solution)/shard_map/pallas_call | solution.py:100
  2.1 8.3 %collective-permute-start.1 = (bf16[768,1152]{1,0:T(8,128)(2,1)S(1)}, bf16[768,1152]{1,0:T(8,128)(2,1)S(1)}, u32[]{:S(2)}, u32[]{:S(2)}) collective-permute-start(bf16[768,1152]{1,0:T(8,128)(2,1)S(1)} %shard_map.59.first_ref.refs_0_), channel_id=1, source_target_pairs={{0,255},{1,2},{2,1},{3,4},{4,3},{5,6},{6,5},{7,8},{8,7},{9,10},{10... | collective-permute-start | bytes 5308424 | tf_op jit(solution)/shard_map/ppermute | solution.py:405
  11.1 0.0 copy-done
  11.1 4.2 %shard_map.60 = (bf16[512,1152]{1,0:T(8,128)(2,1)S(1)}, bf16[512,1152]{1,0:T(8,128)(2,1)S(1)}, bf16[256,1152]{1,0:T(8,128)(2,1)S(1)}, f32[1024,1152]{1,0:T(8,128...) custom-call(bf16[1024,1152]{1,0:T(8,128)(2,1)} %images_ref.3, bf16[1024,1152]{1,0:T(8,128)(2,1)} %texts_ref.3, ...), custom_call_target="tpu_custom_call" | custom-call | flops 3623878656 | tf_op jit(solution)/shard_map/pallas_call | solution.py:176
  15.3 0.1 collective-permute-start.2
  15.4 0.5 %collective-permute-start.3 = (bf16[512,1152]{1,0:T(8,128)(2,1)S(1)}, bf16[512,1152]{1,0:T(8,128)(2,1)S(1)}, u32[]{:S(2)}, u32[]{:S(2)}) collective-permute-start(bf16[512,1152]{1,0:T(8,128)(2,1)S(1)} %get-tuple-element.24.refs_1_.refs_3_), channel_id=1, source_target_pairs={{0,1},{1,0},{2,3},{3,2},{4,5},{5,4},{6,7},{7,6},{8,9},{9,8},{10,11... | collective-permute-start | bytes 3538952 | tf_op jit(solution)/shard_map/ppermute | solution.py:406
  15.9 2.5 %shard_map.61 = (bf16[256,1152]{1,0:T(8,128)(2,1)S(1)}, f32[1024,1152]{1,0:T(8,128)S(1)}, f32[1024,1152]{1,0:T(8,128)S(1)}) custom-call(s32[1,1024]{1,0:T(1,128)S(1)} %bitcast.4, bf16[768,1152]{1,0:T(8,128)(2,1)S(1)} %shard_map.59.first_ref.refs_0_, ...), custom_call_target="tpu_custom_call", output_to_operand_aliasing={{0}: (2, {}), {1}: (5, {}), {2}: (6, {})} | custom-call | flops 1811939328 | tf_op jit(solution)/shard_map/pallas_call | solution.py:224
  18.4 0.3 collective-permute-start
  18.7 4.5 %shard_map.62 = (f32[1024,1152]{1,0:T(8,128)S(1)}, f32[1024,1152]{1,0:T(8,128)S(1)}) custom-call(s32[1,1024]{1,0:T(1,128)S(1)} %bitcast.5, bf16[768,1152]{1,0:T(8,128)(2,1)S(1)} %shard_map.59.first_ref.refs_0_, bf16[256,1152]{1,0:T(8,128)(2,1)S(1)} %get-tuple-element.27.refs_1_, ...), custom_call_target="tpu_custom_call", output_to_operand_aliasing={{0}: (5, {}), {1}: (6, {})} | custom-call | flops 3623878656 | tf_op jit(solution)/shard_map/pallas_call | solution.py:201
  23.2 0.0 collective-permute-done.2.refs_2_
  23.2 0.0 collective-permute-done.3.refs_3_
  23.2 6.2 %shard_map.63 = (f32[1024,1152]{1,0:T(8,128)S(1)}, bf16[1024,1152]{1,0:T(8,128)(2,1)S(1)}) custom-call(bf16[512,1152]{1,0:T(8,128)(2,1)S(1)} %get-tuple-element.23.refs_0_.refs_2_, bf16[512,1152]{1,0:T(8,128)(2,1)S(1)} %get-tuple-element.24.refs_1_.refs_3_, bf16[512,1152]{1,0:T(8,128)(2,1)S(1)} %collective-permute-done.2.refs_2_, ...), custom_call_target="tpu_custom_call" | custom-call | flops 4831838208 | tf_op jit(solution)/shard_map/pallas_call | solution.py:283
  29.4 1.2 %collective-permute-done.1.refs_2_ = bf16[768,1152]{1,0:T(8,128)(2,1)S(1)} collective-permute-done((bf16[768,1152]{1,0:T(8,128)(2,1)S(1)}, bf16[768,1152]{1,0:T(8,128)(2,1)S(1)}, u32[]{:S(2)}, u32[]{:S(2)}) %collective-permute-start.1) | collective-permute-done | bytes 1769504 | tf_op jit(solution)/shard_map/ppermute | solution.py:405
  30.6 5.9 %shard_map.64 = (f32[1024,1152]{1,0:T(8,128)S(1)}, bf16[1024,1152]{1,0:T(8,128)(2,1)}, f32[1024,1152]{1,0:T(8,128)}) custom-call(bf16[768,1152]{1,0:T(8,128)(2,1)S(1)} %shard_map.59.first_ref.refs_0_, bf16[256,1152]{1,0:T(8,128)(2,1)S(1)} %get-tuple-element.27.refs_1_, ...), custom_call_target="tpu_custom_call", output_to_operand_aliasing={{0}: (3, {})} | custom-call | flops 3623878656 | tf_op jit(solution)/shard_map/pallas_call | solution.py:368
  36.5 0.4 %collective-permute-done.refs_2_ = bf16[256,1152]{1,0:T(8,128)(2,1)S(1)} collective-permute-done((bf16[256,1152]{1,0:T(8,128)(2,1)S(1)}, bf16[256,1152]{1,0:T(8,128)(2,1)S(1)}, u32[]{:S(2)}, u32[]{:S(2)}) %collective-permute-start) | collective-permute-done | bytes 589856 | tf_op jit(solution)/shard_map/ppermute | solution.py:405
  36.9 2.7 %shard_map.65 = (bf16[1024,1152]{1,0:T(8,128)(2,1)}, f32[1024,1152]{1,0:T(8,128)}) custom-call(bf16[768,1152]{1,0:T(8,128)(2,1)S(1)} %shard_map.59.first_ref.refs_0_, bf16[256,1152]{1,0:T(8,128)(2,1)S(1)} %get-tuple-element.27.refs_1_, bf16[256,1152]{1,0:T(8,128)(2,1)S(1)} %collective-permute-done.refs_2_, ...), custom_call_target="tpu_custom_call", output_to_operand_aliasing={{0}: (5, {}), {1}: (6, {})} | custom-call | flops 1207959552 | tf_op jit(solution)/shard_map/pallas_call | solution.py:320
Async XLA Ops:
  0.6 10.4 %copy-start = (s32[1024]{0:T(1024)S(1)}, s32[1024]{0:T(1024)}, u32[]{:S(2)}) copy-start(s32[1024]{0:T(1024)} %param.6) | copy-start | bytes 12292
  2.1 28.5 %collective-permute-start.1 = (bf16[768,1152]{1,0:T(8,128)(2,1)S(1)}, bf16[768,1152]{1,0:T(8,128)(2,1)S(1)}, u32[]{:S(2)}, u32[]{:S(2)}) collective-permute-start(bf16[768,1152]{1,0:T(8,128)(2,1)S(1)} %shard_map.59.first_ref.refs_0_), channel_id=1, source_target_pairs={{0,255},{1,2},{2,1},{3,4},{4,3},{5,6},{6,5},{7,8},{8,7},{9,10},{10... | collective-permute-start | bytes 5308424 | tf_op jit(solution)/shard_map/ppermute | solution.py:405
  15.3 7.9 %collective-permute-start.2 = (bf16[512,1152]{1,0:T(8,128)(2,1)S(1)}, bf16[512,1152]{1,0:T(8,128)(2,1)S(1)}, u32[]{:S(2)}, u32[]{:S(2)}) collective-permute-start(bf16[512,1152]{1,0:T(8,128)(2,1)S(1)} %get-tuple-element.23.refs_0_.refs_2_), channel_id=1, source_target_pairs={{0,1},{1,0},{2,3},{3,2},{4,5},{5,4},{6,7},{7,6},{8,9},{9,8},{10,11... | collective-permute-start | bytes 3538952 | tf_op jit(solution)/shard_map/ppermute | solution.py:406
  15.4 7.8 %collective-permute-start.3 = (bf16[512,1152]{1,0:T(8,128)(2,1)S(1)}, bf16[512,1152]{1,0:T(8,128)(2,1)S(1)}, u32[]{:S(2)}, u32[]{:S(2)}) collective-permute-start(bf16[512,1152]{1,0:T(8,128)(2,1)S(1)} %get-tuple-element.24.refs_1_.refs_3_), channel_id=1, source_target_pairs={{0,1},{1,0},{2,3},{3,2},{4,5},{5,4},{6,7},{7,6},{8,9},{9,8},{10,11... | collective-permute-start | bytes 3538952 | tf_op jit(solution)/shard_map/ppermute | solution.py:406
  18.4 18.5 %collective-permute-start = (bf16[256,1152]{1,0:T(8,128)(2,1)S(1)}, bf16[256,1152]{1,0:T(8,128)(2,1)S(1)}, u32[]{:S(2)}, u32[]{:S(2)}) collective-permute-start(bf16[256,1152]{1,0:T(8,128)(2,1)S(1)} %get-tuple-element.27.refs_1_), channel_id=1, source_target_pairs={{0,255},{1,2},{2,1},{3,4},{4,3},{5,6},{6,5},{7,8},{8,7},{9,10},{10... | collective-permute-start | bytes 1769480 | tf_op jit(solution)/shard_map/ppermute | solution.py:405

commit v5 on v4

--- a/solution.py
+++ b/solution.py
@@ -16,7 +16,7 @@
 EVEN_HEAD = 1
 ODD_HEAD = 2
 LAST_TILE = 256
-PICK_TILE = 128
+PICK_TILE = 256
 PAIR_TILE = 512
 NT = (((1,), (1,)), ((), ()))
 NN = (((1,), (0,)), ((), ()))
@@ -375,7 +375,7 @@
         in_specs=[VMEM] * (n + parts + 3),
         out_specs=(VMEM, ANY, ANY),
         scratch_shapes=[pltpu.SemaphoreType.DMA((4,))],
-        input_output_aliases={n + parts: 0},
+
         compiler_params=params(16),
         cost_estimate=cost(2, rows, sum(o.shape[0] for o in other), depth),
     )(*[in_vmem(o) for o in (*own, *other, acc, *done)])

time: 40 us -> 39.9 us (level)
  Pallas kernels: 27.5 us -> 26.8 us
  waiting for transfers between devices: 1.63 us -> 2.21 us
    ppermute x2, waiting for transfers between devices: 1.62 us -> 2.21 us  [local(): far = [lax.ppermute(part, 'dp', far_pairs) for part in far_own]]
  transfers between devices with their start and end apart: 4 -> 4, of which waited for: 2 -> 2; matrix products, arithmetic and copies ran while one was open for 0% -> 0% of each run, Pallas kernels for 59% -> 57%
where the time goes in v5:
time: 39.9 us; the launch traced here: 39.7 us
  Pallas kernels  26.8 us (67%)
  starting transfers between devices  9.16 us (23%)
  waiting for transfers between devices  2.21 us (6%)
  between operations  1.56 us (4%)
    ppermute x2, starting transfers between devices, local(): far = [lax.ppermute(part, 'dp', far_pairs) for part in far_own]  8.57 us
    pallas_call x1, Pallas kernels, near_pair(): pl.pallas_call(functools.partial(near_kernel, n), out_shape=(pltpu.VMEM((...  6.12 us
    pallas_call x1, Pallas kernels, middle(): pl.pallas_call(functools.partial(middle_kernel, n, parts), out_shape=(plt...  5.56 us
    pallas_call x1, Pallas kernels, own_rest(): pl.pallas_call(functools.partial(rest_kernel, n), out_shape=(pltpu.VMEM((...  4.39 us
    pallas_call x1, Pallas kernels, own_head(): pl.pallas_call(functools.partial(head_kernel, wanted, bases), out_shape=(...  4.18 us
    pallas_call x1, Pallas kernels, last(): pl.pallas_call(functools.partial(last_kernel, n, tile), out_shape=(jax.Sh...  2.64 us
    pallas_call x1, Pallas kernels, catch_up(): pl.pallas_call(catch_up_kernel, out_shape=(pltpu.VMEM(later.shape, later....  2.47 us
    ppermute x2, waiting for transfers between devices, local(): far = [lax.ppermute(part, 'dp', far_pairs) for part in far_own]  2.21 us
  transfers between devices with their start and end apart: 4, of which 2 were waited for; matrix products, arithmetic and copies ran while one was open for 0% of the time, Pallas kernels for 57%

profile of v5, /device:TPU:0, one launch (start us, length us, event | category | flops | bytes accessed | tf_op | source)
XLA Modules:
  0.0 39.7 jit_solution(4880591803197555443)
XLA Ops:
  0.6 0.0 copy-start
  0.6 1.5 %shard_map.59.first_ref.refs_0_ = bf16[768,1152]{1,0:T(8,128)(2,1)S(1)} custom-call(bf16[1024,1152]{1,0:T(8,128)(2,1)} %images_ref.3, bf16[1024,1152]{1,0:T(8,128)(2,1)} %texts_ref.3), custom_call_target="tpu_custom_call" | custom-call | tf_op jit(solution)/shard_map/pallas_call | solution.py:100
  2.1 8.3 %collective-permute-start.1 = (bf16[768,1152]{1,0:T(8,128)(2,1)S(1)}, bf16[768,1152]{1,0:T(8,128)(2,1)S(1)}, u32[]{:S(2)}, u32[]{:S(2)}) collective-permute-start(bf16[768,1152]{1,0:T(8,128)(2,1)S(1)} %shard_map.59.first_ref.refs_0_), channel_id=1, source_target_pairs={{0,255},{1,2},{2,1},{3,4},{4,3},{5,6},{6,5},{7,8},{8,7},{9,10},{10... | collective-permute-start | bytes 5308424 | tf_op jit(solution)/shard_map/ppermute | solution.py:405
  11.0 0.0 copy-done
  11.1 4.2 %shard_map.60 = (bf16[512,1152]{1,0:T(8,128)(2,1)S(1)}, bf16[512,1152]{1,0:T(8,128)(2,1)S(1)}, bf16[256,1152]{1,0:T(8,128)(2,1)S(1)}, f32[1024,1152]{1,0:T(8,128...) custom-call(bf16[1024,1152]{1,0:T(8,128)(2,1)} %images_ref.3, bf16[1024,1152]{1,0:T(8,128)(2,1)} %texts_ref.3, ...), custom_call_target="tpu_custom_call" | custom-call | flops 3623878656 | tf_op jit(solution)/shard_map/pallas_call | solution.py:176
  15.2 0.1 collective-permute-start.2
  15.3 0.5 %collective-permute-start.3 = (bf16[512,1152]{1,0:T(8,128)(2,1)S(1)}, bf16[512,1152]{1,0:T(8,128)(2,1)S(1)}, u32[]{:S(2)}, u32[]{:S(2)}) collective-permute-start(bf16[512,1152]{1,0:T(8,128)(2,1)S(1)} %get-tuple-element.24.refs_1_.refs_3_), channel_id=1, source_target_pairs={{0,1},{1,0},{2,3},{3,2},{4,5},{5,4},{6,7},{7,6},{8,9},{9,8},{10,11... | collective-permute-start | bytes 3538952 | tf_op jit(solution)/shard_map/ppermute | solution.py:406
  15.8 2.5 %shard_map.61 = (bf16[256,1152]{1,0:T(8,128)(2,1)S(1)}, f32[1024,1152]{1,0:T(8,128)S(1)}, f32[1024,1152]{1,0:T(8,128)S(1)}) custom-call(s32[1,1024]{1,0:T(1,128)S(1)} %bitcast.4, bf16[768,1152]{1,0:T(8,128)(2,1)S(1)} %shard_map.59.first_ref.refs_0_, ...), custom_call_target="tpu_custom_call", output_to_operand_aliasing={{0}: (2, {}), {1}: (5, {}), {2}: (6, {})} | custom-call | flops 1811939328 | tf_op jit(solution)/shard_map/pallas_call | solution.py:224
  18.3 0.3 collective-permute-start
  18.6 4.4 %shard_map.62 = (f32[1024,1152]{1,0:T(8,128)S(1)}, f32[1024,1152]{1,0:T(8,128)S(1)}) custom-call(s32[1,1024]{1,0:T(1,128)S(1)} %bitcast.5, bf16[768,1152]{1,0:T(8,128)(2,1)S(1)} %shard_map.59.first_ref.refs_0_, bf16[256,1152]{1,0:T(8,128)(2,1)S(1)} %get-tuple-element.27.refs_1_, ...), custom_call_target="tpu_custom_call", output_to_operand_aliasing={{0}: (5, {}), {1}: (6, {})} | custom-call | flops 3623878656 | tf_op jit(solution)/shard_map/pallas_call | solution.py:201
  23.0 0.0 collective-permute-done.2.refs_2_
  23.0 0.0 collective-permute-done.3.refs_3_
  23.0 6.1 %shard_map.63 = (f32[1024,1152]{1,0:T(8,128)S(1)}, bf16[1024,1152]{1,0:T(8,128)(2,1)S(1)}) custom-call(bf16[512,1152]{1,0:T(8,128)(2,1)S(1)} %get-tuple-element.23.refs_0_.refs_2_, bf16[512,1152]{1,0:T(8,128)(2,1)S(1)} %get-tuple-element.24.refs_1_.refs_3_, bf16[512,1152]{1,0:T(8,128)(2,1)S(1)} %collective-permute-done.2.refs_2_, ...), custom_call_target="tpu_custom_call" | custom-call | flops 4831838208 | tf_op jit(solution)/shard_map/pallas_call | solution.py:283
  29.1 1.5 %collective-permute-done.1.refs_2_ = bf16[768,1152]{1,0:T(8,128)(2,1)S(1)} collective-permute-done((bf16[768,1152]{1,0:T(8,128)(2,1)S(1)}, bf16[768,1152]{1,0:T(8,128)(2,1)S(1)}, u32[]{:S(2)}, u32[]{:S(2)}) %collective-permute-start.1) | collective-permute-done | bytes 1769504 | tf_op jit(solution)/shard_map/ppermute | solution.py:405
  30.6 5.6 %shard_map.64 = (f32[1024,1152]{1,0:T(8,128)S(1)}, bf16[1024,1152]{1,0:T(8,128)(2,1)}, f32[1024,1152]{1,0:T(8,128)}) custom-call(bf16[768,1152]{1,0:T(8,128)(2,1)S(1)} %shard_map.59.first_ref.refs_0_, bf16[256,1152]{1,0:T(8,128)(2,1)S(1)} %get-tuple-element.27.refs_1_, bf16[768,1152]{1,0:T(8,128)(2,1)S(1)} %collective-permute-done.1.refs_2_, ...), custom_call_target="tpu_custom_call" | custom-call | flops 3623878656 | tf_op jit(solution)/shard_map/pallas_call | solution.py:368
  36.2 0.8 %collective-permute-done.refs_2_ = bf16[256,1152]{1,0:T(8,128)(2,1)S(1)} collective-permute-done((bf16[256,1152]{1,0:T(8,128)(2,1)S(1)}, bf16[256,1152]{1,0:T(8,128)(2,1)S(1)}, u32[]{:S(2)}, u32[]{:S(2)}) %collective-permute-start) | collective-permute-done | bytes 589856 | tf_op jit(solution)/shard_map/ppermute | solution.py:405
  36.9 2.6 %shard_map.65 = (bf16[1024,1152]{1,0:T(8,128)(2,1)}, f32[1024,1152]{1,0:T(8,128)}) custom-call(bf16[768,1152]{1,0:T(8,128)(2,1)S(1)} %shard_map.59.first_ref.refs_0_, bf16[256,1152]{1,0:T(8,128)(2,1)S(1)} %get-tuple-element.27.refs_1_, bf16[256,1152]{1,0:T(8,128)(2,1)S(1)} %collective-permute-done.refs_2_, ...), custom_call_target="tpu_custom_call", output_to_operand_aliasing={{0}: (5, {}), {1}: (6, {})} | custom-call | flops 1207959552 | tf_op jit(solution)/shard_map/pallas_call | solution.py:320
Async XLA Ops:
  0.6 10.4 %copy-start = (s32[1024]{0:T(1024)S(1)}, s32[1024]{0:T(1024)}, u32[]{:S(2)}) copy-start(s32[1024]{0:T(1024)} %param.6) | copy-start | bytes 12292
  2.1 28.5 %collective-permute-start.1 = (bf16[768,1152]{1,0:T(8,128)(2,1)S(1)}, bf16[768,1152]{1,0:T(8,128)(2,1)S(1)}, u32[]{:S(2)}, u32[]{:S(2)}) collective-permute-start(bf16[768,1152]{1,0:T(8,128)(2,1)S(1)} %shard_map.59.first_ref.refs_0_), channel_id=1, source_target_pairs={{0,255},{1,2},{2,1},{3,4},{4,3},{5,6},{6,5},{7,8},{8,7},{9,10},{10... | collective-permute-start | bytes 5308424 | tf_op jit(solution)/shard_map/ppermute | solution.py:405
  15.2 7.8 %collective-permute-start.2 = (bf16[512,1152]{1,0:T(8,128)(2,1)S(1)}, bf16[512,1152]{1,0:T(8,128)(2,1)S(1)}, u32[]{:S(2)}, u32[]{:S(2)}) collective-permute-start(bf16[512,1152]{1,0:T(8,128)(2,1)S(1)} %get-tuple-element.23.refs_0_.refs_2_), channel_id=1, source_target_pairs={{0,1},{1,0},{2,3},{3,2},{4,5},{5,4},{6,7},{7,6},{8,9},{9,8},{10,11... | collective-permute-start | bytes 3538952 | tf_op jit(solution)/shard_map/ppermute | solution.py:406
  15.3 7.7 %collective-permute-start.3 = (bf16[512,1152]{1,0:T(8,128)(2,1)S(1)}, bf16[512,1152]{1,0:T(8,128)(2,1)S(1)}, u32[]{:S(2)}, u32[]{:S(2)}) collective-permute-start(bf16[512,1152]{1,0:T(8,128)(2,1)S(1)} %get-tuple-element.24.refs_1_.refs_3_), channel_id=1, source_target_pairs={{0,1},{1,0},{2,3},{3,2},{4,5},{5,4},{6,7},{7,6},{8,9},{9,8},{10,11... | collective-permute-start | bytes 3538952 | tf_op jit(solution)/shard_map/ppermute | solution.py:406
  18.3 18.6 %collective-permute-start = (bf16[256,1152]{1,0:T(8,128)(2,1)S(1)}, bf16[256,1152]{1,0:T(8,128)(2,1)S(1)}, u32[]{:S(2)}, u32[]{:S(2)}) collective-permute-start(bf16[256,1152]{1,0:T(8,128)(2,1)S(1)} %get-tuple-element.27.refs_1_), channel_id=1, source_target_pairs={{0,255},{1,2},{2,1},{3,4},{4,3},{5,6},{6,5},{7,8},{8,7},{9,10},{10... | collective-permute-start | bytes 1769480 | tf_op jit(solution)/shard_map/ppermute | solution.py:405
